TPU v7x, 256 devices: a whole 4x4x8 slice. The times are simulated.
256 devices in a mesh: dp: 32 (over z_lo, x, y), tensor: 8 (over z_hi, core).
Axes of the slice: x: 4, y: 4, z: 8 (z_hi: 4, z_lo: 2; z = z_hi * 2 + z_lo), core: 2. Of those that a mesh axis runs over, the one named last changes fastest.
Arguments:
- encoder_input_states: bfloat16 [32, 64, 4096], P('dp', None, 'tensor'), may hold values from -6 to 6
- caption_lengths: int32 [32], P('dp'), may hold values from 16 to 64
- encoder_input_gain: float32 [4096], replicated, may hold values from 0.1 to 1.9
- query_head_gain: float32 [128], replicated, may hold values from 0.1 to 1.9
- key_head_gain: float32 [128], replicated, may hold values from 0.1 to 1.9
- encoder_query_weight: bfloat16 [4096, 4096], P(None, 'tensor'), may hold values from -0.09375 to 0.09375
- encoder_key_weight: bfloat16 [4096, 1024], P(None, 'tensor'), may hold values from -0.09375 to 0.09375
- encoder_value_weight: bfloat16 [4096, 1024], P(None, 'tensor'), may hold values from -0.09375 to 0.09375
- encoder_output_weight: bfloat16 [4096, 4096], P('tensor'), may hold values from -0.09375 to 0.09375
- clean_motion: bfloat16 [32, 360, 256], P('dp'), may hold values from -15 to 15
- noise: bfloat16 [32, 360, 256], P('dp'), may hold values from -15 to 15
- timestep_index: int32 [32], P('dp'), may hold values from 0 to 999
- motion_lengths: int32 [32], P('dp'), may hold values from 90 to 360
- input_weight: bfloat16 [256, 2048], P(None, 'dp'), may hold values from -0.375 to 0.375
- velocity_weight: bfloat16 [2048, 256], P('dp'), may hold values from -0.125 to 0.125
- cross_query_weight: bfloat16 [2048, 2048], P('dp', 'tensor'), may hold values from -0.125 to 0.125
- cross_key_weight: bfloat16 [4096, 2048], P('dp', 'tensor'), may hold values from -0.09375 to 0.09375
- cross_value_weight: bfloat16 [4096, 2048], P('dp', 'tensor'), may hold values from -0.09375 to 0.09375
- cross_output_weight: bfloat16 [2048, 2048], P('tensor', 'dp'), may hold values from -0.125 to 0.125
Outputs:
- loss: float32 [], replicated
- grad_wq: float32 [2048, 2048], P('dp', 'tensor')
- grad_wk: float32 [4096, 2048], P('dp', 'tensor')
- grad_wv: float32 [4096, 2048], P('dp', 'tensor')
- grad_wo: float32 [2048, 2048], P('tensor', 'dp')
Inputs may be any that keep to these rules, and one draw needn't show every extreme that they name: caption tokens from index caption_lengths on are padding. Frames from index motion_lengths on are padding.
All inputs are finite; a program needn't handle non-finite values.
Results may differ from a plain program's by a relative error of at most 0.04.
Values may be sent and summed in bfloat16 or wider, within the bound.
A program may use at most 128 MiB of HBM per device.

v0:
```python
import math

import jax
import jax.numpy as jnp
from jax import lax
from jax.sharding import PartitionSpec as P

STEPS = 1000


EPSILON = 1e-06


def rope_tables(sequence_length, size_of_head):
    halfway = size_of_head // 2
    inverse = 1000000.0 ** (-(jnp.arange(halfway, dtype=jnp.float32) * 2.0 / size_of_head))
    angles = jnp.arange(sequence_length, dtype=jnp.float32)[:, None] * inverse[None, :]
    angles = jnp.concatenate([angles, angles], axis=1)
    return (jnp.cos(angles)[:, None, :], jnp.sin(angles)[:, None, :])


def rotate(vectors, cosine, sine_table):
    halfway = vectors.shape[-1] // 2
    turned = jnp.concatenate([-vectors[..., halfway:], vectors[..., :halfway]], axis=-1)
    return vectors * cosine + turned * sine_table


def head_norm(vectors, scaling):
    return (
        vectors * lax.rsqrt(jnp.mean(vectors * vectors, axis=-1, keepdims=True) + EPSILON) * scaling
    )


def encode_heads(
    gathered,
    caption_lengths,
    encoder_input_gain,
    query_head_gain,
    key_head_gain,
    encoder_query_weight,
    encoder_key_weight,
    encoder_value_weight,
    encoder_output_weight,
):
    total_number, sequence_length, model_width = gathered.shape
    size_of_head = query_head_gain.shape[0]
    widened = gathered.astype(jnp.float32)
    normalized_rows = (
        widened
        * lax.rsqrt(jnp.mean(widened * widened, axis=-1, keepdims=True) + EPSILON)
        * encoder_input_gain
    ).astype(jnp.bfloat16)
    flattened_rows = normalized_rows.reshape(total_number * sequence_length, model_width)
    query_heads = encoder_query_weight.shape[1] // size_of_head
    kv_heads = encoder_key_weight.shape[1] // size_of_head
    cosine, sine_table = rope_tables(sequence_length, size_of_head)
    query_matrix = jnp.dot(
        flattened_rows, encoder_query_weight, preferred_element_type=jnp.float32
    ).reshape(total_number, sequence_length, query_heads, size_of_head)
    query_matrix = rotate(head_norm(query_matrix, query_head_gain), cosine, sine_table).astype(
        jnp.bfloat16
    )
    key_matrix = jnp.dot(
        flattened_rows, encoder_key_weight, preferred_element_type=jnp.float32
    ).reshape(total_number, sequence_length, kv_heads, size_of_head)
    key_matrix = rotate(head_norm(key_matrix, key_head_gain), cosine, sine_table).astype(
        jnp.bfloat16
    )
    value_matrix = (
        jnp.dot(flattened_rows, encoder_value_weight, preferred_element_type=jnp.float32)
        .astype(jnp.bfloat16)
        .reshape(total_number, sequence_length, kv_heads, size_of_head)
    )
    repeats = query_heads // kv_heads
    key_matrix = jnp.repeat(key_matrix, repeats, axis=2)
    value_matrix = jnp.repeat(value_matrix, repeats, axis=2)
    scores = jnp.einsum(
        "mqhd,mkhd->mhqk", query_matrix, key_matrix, preferred_element_type=jnp.float32
    ) / math.sqrt(size_of_head)
    position = jnp.arange(sequence_length, dtype=jnp.int32)
    causal = position[None, :] <= position[:, None]
    padding = position[None, :] < caption_lengths[:, None]
    allowed = causal[None, None, :, :] & padding[:, None, None, :]
    scores = jnp.where(allowed, scores, -1e30)
    weights = jax.nn.softmax(scores, axis=-1).astype(jnp.bfloat16)
    attended_rows = jnp.einsum(
        "mhqk,mkhd->mqhd", weights, value_matrix, preferred_element_type=jnp.float32
    ).astype(jnp.bfloat16)
    attended_rows = attended_rows.reshape(
        total_number * sequence_length, query_heads * size_of_head
    )
    return jnp.dot(attended_rows, encoder_output_weight, preferred_element_type=jnp.float32)


def timestep_embedding(timestep_index, model_width):
    halfway = model_width // 2
    frequency = jnp.exp(-math.log(10000.0) * jnp.arange(halfway, dtype=jnp.float32) / halfway)
    angles = timestep_index.astype(jnp.float32)[:, None] * frequency[None, :]
    return jnp.concatenate([jnp.cos(angles), jnp.sin(angles)], axis=1)


def contract_rows(left, right):
    return lax.dot_general(
        left, right, (((0,), (0,)), ((), ())), preferred_element_type=jnp.float32
    )


def local(
    encoder_input_states,
    caption_lengths,
    encoder_input_gain,
    query_head_gain,
    key_head_gain,
    encoder_query_weight,
    encoder_key_weight,
    encoder_value_weight,
    encoder_output_weight,
    clean_motion,
    noise,
    timestep_index,
    motion_lengths,
    input_weight,
    velocity_weight,
    cross_query_weight,
    cross_key_weight,
    cross_value_weight,
    cross_output_weight,
):
    size_of_head = query_head_gain.shape[0]
    gathered = lax.all_gather(encoder_input_states, "tensor", axis=2, tiled=True)
    total_number, sequence_length, text_width = gathered.shape
    partial_value = encode_heads(
        gathered,
        caption_lengths,
        encoder_input_gain,
        query_head_gain,
        key_head_gain,
        encoder_query_weight,
        encoder_key_weight,
        encoder_value_weight,
        encoder_output_weight,
    )
    summed = lax.psum(partial_value.astype(jnp.bfloat16), "tensor").astype(jnp.float32)
    caption_hidden = (
        gathered.astype(jnp.float32) + summed.reshape(total_number, sequence_length, text_width)
    ).astype(jnp.bfloat16)
    query_all, key_all, value_all, velocity_all = (
        lax.all_gather(cross_query_weight, "dp", axis=0, tiled=True),
        lax.all_gather(cross_key_weight, "dp", axis=0, tiled=True),
        lax.all_gather(cross_value_weight, "dp", axis=0, tiled=True),
        lax.all_gather(velocity_weight, "dp", axis=0, tiled=True),
    )
    output_all, input_all = (
        lax.all_gather(cross_output_weight, "dp", axis=1, tiled=True),
        lax.all_gather(input_weight, "dp", axis=1, tiled=True),
    )
    frame_count = clean_motion.shape[1]
    channels = clean_motion.shape[2]
    row_count = total_number * frame_count
    model_width = input_all.shape[1]
    flow_time = timestep_index.astype(jnp.float32)[:, None, None] / STEPS
    clean = clean_motion.astype(jnp.float32)
    noisy = noise.astype(jnp.float32)
    blended = ((1.0 - flow_time) * clean + flow_time * noisy).astype(jnp.bfloat16)
    target = (noisy - clean).reshape(row_count, channels)
    hidden = jnp.dot(
        blended.reshape(row_count, channels), input_all, preferred_element_type=jnp.float32
    ).reshape(total_number, frame_count, model_width)
    hidden = (hidden + timestep_embedding(timestep_index, model_width)[:, None, :]).reshape(
        row_count, model_width
    )
    centered = hidden - jnp.mean(hidden, axis=-1, keepdims=True)
    normalized_rows = (
        centered * lax.rsqrt(jnp.mean(centered * centered, axis=-1, keepdims=True) + EPSILON)
    ).astype(jnp.bfloat16)
    count_of_heads = query_all.shape[1] // size_of_head
    flattened_rows = caption_hidden.reshape(total_number * sequence_length, text_width)
    query_matrix = (
        jnp.dot(normalized_rows, query_all, preferred_element_type=jnp.float32)
        .astype(jnp.bfloat16)
        .reshape(total_number, frame_count, count_of_heads, size_of_head)
    )
    key_matrix = (
        jnp.dot(flattened_rows, key_all, preferred_element_type=jnp.float32)
        .astype(jnp.bfloat16)
        .reshape(total_number, sequence_length, count_of_heads, size_of_head)
    )
    value_matrix = (
        jnp.dot(flattened_rows, value_all, preferred_element_type=jnp.float32)
        .astype(jnp.bfloat16)
        .reshape(total_number, sequence_length, count_of_heads, size_of_head)
    )
    scaling = 1.0 / math.sqrt(size_of_head)
    scores = (
        jnp.einsum("mfhd,mlhd->mhfl", query_matrix, key_matrix, preferred_element_type=jnp.float32)
        * scaling
    )
    padding = jnp.arange(sequence_length, dtype=jnp.int32)[None, :] < caption_lengths[:, None]
    scores = jnp.where(padding[:, None, None, :], scores, -1e30)
    weights = jax.nn.softmax(scores, axis=-1)
    weights_b = weights.astype(jnp.bfloat16)
    attended_rows = jnp.einsum(
        "mhfl,mlhd->mfhd", weights_b, value_matrix, preferred_element_type=jnp.float32
    ).astype(jnp.bfloat16)
    attended_rows = attended_rows.reshape(row_count, count_of_heads * size_of_head)
    branch_output = jnp.dot(attended_rows, output_all, preferred_element_type=jnp.float32)
    projector = velocity_all.astype(jnp.float32)
    output_rows = hidden + lax.psum(branch_output.astype(jnp.bfloat16), "tensor").astype(
        jnp.float32
    )
    predicted = jnp.dot(output_rows, projector, precision=lax.Precision.HIGHEST)
    residual = predicted - target
    frame_mask = (
        jnp.arange(frame_count, dtype=jnp.int32)[None, :] < motion_lengths[:, None]
    ).astype(jnp.float32)
    row_weight = (frame_mask / motion_lengths.astype(jnp.float32)[:, None]).reshape(row_count, 1)
    loss_part = jnp.sum(residual * residual * row_weight)
    loss = lax.psum(loss_part, "dp") / (total_number * lax.axis_size("dp") * channels)
    d_velocity = 2.0 * residual * row_weight
    output_gradient = jnp.dot(d_velocity, projector.T, precision=lax.Precision.HIGHEST).astype(
        jnp.bfloat16
    )
    output_backward = lax.all_gather(cross_output_weight, "dp", axis=1, tiled=True)
    attended_gradient = lax.dot_general(
        output_gradient,
        output_backward,
        (((1,), (1,)), ((), ())),
        preferred_element_type=jnp.float32,
    )
    attended_gradient = attended_gradient.astype(jnp.bfloat16).reshape(
        total_number, frame_count, count_of_heads, size_of_head
    )
    d_weights = jnp.einsum(
        "mfhd,mlhd->mhfl", attended_gradient, value_matrix, preferred_element_type=jnp.float32
    )
    row_delta = jnp.sum(weights * d_weights, axis=-1, keepdims=True)
    d_scores = (weights * (d_weights - row_delta) * scaling).astype(jnp.bfloat16)
    d_values = jnp.einsum(
        "mhfl,mfhd->mlhd", weights_b, attended_gradient, preferred_element_type=jnp.float32
    ).astype(jnp.bfloat16)
    d_queries = jnp.einsum(
        "mhfl,mlhd->mfhd", d_scores, key_matrix, preferred_element_type=jnp.float32
    ).astype(jnp.bfloat16)
    d_keys = jnp.einsum(
        "mhfl,mfhd->mlhd", d_scores, query_matrix, preferred_element_type=jnp.float32
    ).astype(jnp.bfloat16)
    local_cols = count_of_heads * size_of_head
    d_query_rows = d_queries.reshape(row_count, local_cols)
    d_keyval_rows = jnp.concatenate(
        [
            d_keys.reshape(total_number * sequence_length, local_cols),
            d_values.reshape(total_number * sequence_length, local_cols),
        ],
        axis=1,
    )
    grad_wq = lax.psum_scatter(
        contract_rows(normalized_rows, d_query_rows).astype(jnp.bfloat16),
        "dp",
        scatter_dimension=0,
        tiled=True,
    ).astype(jnp.float32)
    grad_keyval = lax.psum_scatter(
        contract_rows(flattened_rows, d_keyval_rows).astype(jnp.bfloat16),
        "dp",
        scatter_dimension=0,
        tiled=True,
    ).astype(jnp.float32)
    grad_wo = (
        lax.psum_scatter(
            contract_rows(output_gradient, attended_rows).astype(jnp.bfloat16),
            "dp",
            scatter_dimension=0,
            tiled=True,
        )
        .astype(jnp.float32)
        .T
    )
    grad_wk = grad_keyval[:, :local_cols]
    grad_wv = grad_keyval[:, local_cols:]
    return (loss, grad_wq, grad_wk, grad_wv, grad_wo)


def solution(mesh):
    placed = (
        P("dp", None, "tensor"),
        P("dp"),
        P(),
        P(),
        P(),
        P(None, "tensor"),
        P(None, "tensor"),
        P(None, "tensor"),
        P("tensor", None),
        P("dp", None, None),
        P("dp", None, None),
        P("dp"),
        P("dp"),
        P(None, "dp"),
        P("dp", None),
        P("dp", "tensor"),
        P("dp", "tensor"),
        P("dp", "tensor"),
        P("tensor", "dp"),
    )
    return jax.shard_map(
        local,
        mesh=mesh,
        in_specs=placed,
        out_specs=(P(), P("dp", "tensor"), P("dp", "tensor"), P("dp", "tensor"), P("tensor", "dp")),
        check_vma=False,
    )
```

profile of v0, /device:TPU:1, one launch (start us, length us, event | category | flops | bytes accessed | tf_op | source)
XLA Modules:
  0.0 1448.2 jit_solution(8006563809693050161)
XLA Ops:
  9.6 20.3 %all_gather.23 = bf16[1,64,4096]{2,1,0:T(8,128)(2,1)S(1)} all-gather(bf16[1,64,512]{2,1,0:T(8,128)(2,1)} %param.19), channel_id=1, replica_groups=mesh['dp'=32,'tensor'=8] {'tensor'}, dimensions={2}, use_global_device_ids=true | all-gather | bytes 589824 | tf_op jit(solution)/shard_map/all_gather | solution.py:130
  30.1 3.1 fusion.117
  35.8 1.6 convolution_convert_fusion.15
  37.7 3.9 fusion.3
  45.0 103.0 %all-gather.7.cloned.1.call-done = bf16[256,2048]{0,1:T(8,128)(2,1)} async-done(((bf16[256,64]{0,1:T(8,128)(2,1)}), bf16[256,2048]{0,1:T(8,128)(2,1)}) %all-gather.7.cloned.1.call-update) | async-done | bytes 1048592 | tf_op jit(solution)/shard_map/all_gather | solution.py:155
  148.0 1.9 fusion.126
  150.3 1.1 copy-done.1
  151.9 150.4 %all-gather.11.cloned.1.call-done = bf16[2048,256]{1,0:T(8,128)(2,1)} async-done(((bf16[64,256]{1,0:T(8,128)(2,1)}), bf16[2048,256]{1,0:T(8,128)(2,1)}) %all-gather.11.cloned.1.call-update) | async-done | bytes 1048592 | tf_op jit(solution)/shard_map/all_gather | solution.py:148
  302.2 1.8 fusion.17
  304.1 156.9 %all-gather.13.cloned.1.call-done = bf16[4096,256]{1,0:T(8,128)(2,1)} async-done(((bf16[128,256]{1,0:T(8,128)(2,1)}), bf16[4096,256]{1,0:T(8,128)(2,1)}) %all-gather.13.cloned.1.call-update) | async-done | bytes 2097168 | tf_op jit(solution)/shard_map/all_gather | solution.py:149
  461.0 2.2 fusion.28
  463.4 0.7 fusion.127
  464.1 154.4 %all-gather.9.cloned.1.call-done = bf16[4096,256]{1,0:T(8,128)(2,1)} async-done(((bf16[128,256]{1,0:T(8,128)(2,1)}), bf16[4096,256]{1,0:T(8,128)(2,1)}) %all-gather.9.cloned.1.call-update) | async-done | bytes 2097168 | tf_op jit(solution)/shard_map/all_gather | solution.py:150
  618.5 2.0 fusion.27
  621.0 151.8 %all-gather.15.cloned.1.call-done = bf16[256,2048]{0,1:T(8,128)(2,1)} async-done(((bf16[256,64]{0,1:T(8,128)(2,1)}), bf16[256,2048]{0,1:T(8,128)(2,1)}) %all-gather.15.cloned.1.call-update) | async-done | bytes 1048592 | tf_op jit(solution)/shard_map/all_gather | solution.py:154
  772.9 3.0 convolution_convert_fusion.3
  776.8 152.8 %all-gather.17.cloned.1.call-done = bf16[2048,256]{1,0:T(8,128)(2,1)} async-done(((bf16[64,256]{1,0:T(8,128)(2,1)}), bf16[2048,256]{1,0:T(8,128)(2,1)}) %all-gather.17.cloned.1.call-update) | async-done | bytes 1048592 | tf_op jit(solution)/shard_map/all_gather | solution.py:151
  929.6 5.0 multiply_reduce_fusion.2
  934.5 1.4 convolution_convert_fusion.2
  935.9 1.1 copy-done.5
  937.9 1.3 fusion.20
  939.4 3.1 convolution_convert_fusion.5
  942.6 3.2 convolution_convert_fusion.4
  945.9 1.2 fusion.25
  947.4 3.2 convolution_convert_fusion
  950.6 70.6 %psum.23 = f32[]{:T(128)} all-reduce(f32[]{:T(128)} %get-tuple-element.22), channel_id=1, replica_groups=mesh['dp'=32,'tensor'=8] {'dp'}, use_global_device_ids=true, to_apply=%region_12.13 | all-reduce | flops 1 | bytes 8 | tf_op jit(solution)/shard_map/psum | solution.py:218
  1021.9 81.0 %reduce-scatter.4.cloned.1.call-done = bf16[64,256]{1,0:T(8,128)(2,1)} async-done(((bf16[2048,256]{1,0:T(8,128)(2,1)}), bf16[64,256]{1,0:T(8,128)(2,1)}) %reduce-scatter.4.cloned.1.call-update) | async-done | bytes 32784 | tf_op jit(solution)/shard_map/reduce_scatter | solution.py:256
  1102.9 1.4 convert_element_type.180
  1104.3 161.2 %reduce-scatter.8.cloned.1.call-done = bf16[64,256]{1,0:T(8,128)(2,1)} async-done(((bf16[2048,256]{1,0:T(8,128)(2,1)}), bf16[64,256]{1,0:T(8,128)(2,1)}) %reduce-scatter.8.cloned.1.call-update) | async-done | bytes 32784 | tf_op jit(solution)/shard_map/reduce_scatter | solution.py:269
  1265.4 1.4 convert_bitcast_fusion
  1266.8 171.5 %reduce-scatter.6.cloned.1.call-done = bf16[128,512]{1,0:T(8,128)(2,1)} async-done(((bf16[4096,512]{1,0:T(8,128)(2,1)}), bf16[128,512]{1,0:T(8,128)(2,1)}) %reduce-scatter.6.cloned.1.call-update) | async-done | bytes 131088 | tf_op jit(solution)/shard_map/reduce_scatter | solution.py:262
  1438.4 1.6 fusion.120
  (98 shorter events, 9.6 us)
Async XLA Ops:
  8.0 25.3 %copy-start = (bf16[4096,128]{1,0:T(8,128)(2,1)S(1)}, bf16[4096,128]{1,0:T(8,128)(2,1)}, u32[]{:S(2)}) copy-start(bf16[4096,128]{1,0:T(8,128)(2,1)} %param.25) | copy-start | bytes 3145732
  8.0 139.9 %all-gather.7.cloned.1.call-start = ((), (), s32[]{:S(2)}) async-start(), calls=%async_computation.3 | async-start | bytes 1081344 | tf_op jit(solution)/shard_map/all_gather | solution.py:155
  8.7 293.5 %all-gather.11.cloned.1.call-start = ((), (), s32[]{:S(2)}) async-start(), calls=%async_computation.6 | async-start | bytes 1081344 | tf_op jit(solution)/shard_map/all_gather | solution.py:148
  9.5 294.6 %all-reduce.3.cloned.1.call-start = ((), (), s32[]{:S(2)}) async-start(), calls=%async_computation.4 | async-start | bytes 1048576 | tf_op jit(solution)/shard_map/psum | solution.py:143
  29.8 3.5 copy-start.15
  30.1 3.7 copy-start.16
  30.1 5.0 copy-start.17
  37.6 110.4 %copy-start.7 = (bf16[1,360,256]{2,1,0:T(8,128)(2,1)S(1)}, bf16[1,360,256]{2,1,0:T(8,128)(2,1)}, u32[]{:S(2)}) copy-start(bf16[1,360,256]{2,1,0:T(8,128)(2,1)} %param.28) | copy-start | bytes 552964
  37.6 110.3 %copy-start.8 = (bf16[1,360,256]{2,1,0:T(8,128)(2,1)S(1)}, bf16[1,360,256]{2,1,0:T(8,128)(2,1)}, u32[]{:S(2)}) copy-start(bf16[1,360,256]{2,1,0:T(8,128)(2,1)} %param.29) | copy-start | bytes 552964
  41.6 419.4 %all-gather.13.cloned.1.call-start = ((), (), s32[]{:S(2)}) async-start(), calls=%async_computation.7 | async-start | bytes 2162688 | tf_op jit(solution)/shard_map/all_gather | solution.py:149
  42.4 576.1 %all-gather.9.cloned.1.call-start = ((), (), s32[]{:S(2)}) async-start(), calls=%async_computation.5 | async-start | bytes 2162688 | tf_op jit(solution)/shard_map/all_gather | solution.py:150
  43.0 729.9 %all-gather.15.cloned.1.call-start = ((), (), s32[]{:S(2)}) async-start(), calls=%async_computation.8 | async-start | bytes 1081344 | tf_op jit(solution)/shard_map/all_gather | solution.py:154
  43.5 886.0 %all-gather.17.cloned.1.call-start = ((), (), s32[]{:S(2)}) async-start(), calls=%async_computation.10 | async-start | bytes 1081344 | tf_op jit(solution)/shard_map/all_gather | solution.py:151
  44.1 885.4 %all-reduce.5.cloned.1.call-start = ((), (), s32[]{:S(2)}) async-start(), calls=%async_computation.9 | async-start | bytes 2949120 | tf_op jit(solution)/shard_map/psum | solution.py:208
  149.9 1.6 copy-start.1
  151.8 152.2 %copy-start.4 = (bf16[360,2048]{1,0:T(8,128)(2,1)}, bf16[360,2048]{1,0:T(8,128)(2,1)S(1)}, u32[]{:S(2)}) copy-start(bf16[360,2048]{1,0:T(8,128)(2,1)S(1)} %multiply_convert_fusion) | copy-start | bytes 4423684
  304.0 316.5 %copy-start.9 = (bf16[45,2,8,128]{3,2,1,0:T(8,128)(2,1)}, bf16[45,2,8,128]{3,2,1,0:T(8,128)(2,1)S(1)}, u32[]{:S(2)}) copy-start(bf16[45,2,8,128]{3,2,1,0:T(8,128)(2,1)S(1)} %fusion.17) | copy-start | bytes 552964
  304.1 314.4 %copy-start.2 = (bf16[1,64,4096]{2,1,0:T(8,128)(2,1)S(1)}, bf16[1,64,4096]{2,1,0:T(8,128)(2,1)}, u32[]{:S(2)}) copy-start(bf16[1,64,4096]{2,1,0:T(8,128)(2,1)} %all-reduce.3.cloned.1.call-done) | copy-start | bytes 1572868
  463.2 157.3 %copy-start.11 = (bf16[8,2,8,128]{3,2,1,0:T(8,128)(2,1)}, bf16[8,2,8,128]{3,2,1,0:T(8,128)(2,1)S(1)}, u32[]{:S(2)}) copy-start(bf16[8,2,8,128]{3,2,1,0:T(8,128)(2,1)S(1)} %fusion.28) | copy-start | bytes 98308
  620.6 156.2 %copy-start.13 = (bf16[8,2,8,128]{3,2,1,0:T(8,128)(2,1)}, bf16[8,2,8,128]{3,2,1,0:T(8,128)(2,1)S(1)}, u32[]{:S(2)}) copy-start(bf16[8,2,8,128]{3,2,1,0:T(8,128)(2,1)S(1)} %fusion.27) | copy-start | bytes 98308
  775.8 327.0 %reduce-scatter.4.cloned.1.call-start = ((), (), s32[]{:S(2)}) async-start(), calls=%async_computation.11 | async-start | bytes 1081344 | tf_op jit(solution)/shard_map/reduce_scatter | solution.py:256
  929.6 5.0 copy-start.3
  929.6 7.5 copy-start.6
  934.5 3.1 copy-start.14
  935.9 1.1 copy-start.5
  937.0 0.8 copy-start.12
  942.5 3.4 copy-start.10
  942.5 322.9 %reduce-scatter.8.cloned.1.call-start = ((), (), s32[]{:S(2)}) async-start(), calls=%async_computation.13 | async-start | bytes 1081344 | tf_op jit(solution)/shard_map/reduce_scatter | solution.py:269
  945.8 492.6 %reduce-scatter.6.cloned.1.call-start = ((), (), s32[]{:S(2)}) async-start(), calls=%async_computation.12 | async-start | bytes 4325376 | tf_op jit(solution)/shard_map/reduce_scatter | solution.py:262
Sparse Core Ops, SparseCore 0:
  10.6 137.2 all-gather.6
  149.7 152.4 all-gather.10
  304.0 156.9 all-gather.12
  462.6 155.8 all-gather.8
  620.1 152.6 all-gather.14
  774.5 155.0 all-gather.16
  942.6 160.1 reduce-scatter.3
  1105.4 160.0 reduce-scatter.7
  1268.1 170.1 reduce-scatter.5
Sparse Core Ops, SparseCore 1:
  41.7 72.7 all-reduce.2
  775.9 102.1 all-reduce.4
where the time goes:
time: 1470 us; the launch traced here: 1450 us
  waiting for transfers between devices  1290 us (88%)
  blocking collectives  90.9 us (6%)
  matrix products  40.3 us (3%)
  between operations  19.5 us (1%)
    reduce_scatter x1, waiting for transfers between devices, local(): lax.psum_scatter(contract_rows(flattened_rows, d_keyval_rows).astype(jnp....  172 us
    reduce_scatter x1, waiting for transfers between devices, local(): lax.psum_scatter(contract_rows(output_gradient, attended_rows).astype(jnp...  161 us
    all_gather x1, waiting for transfers between devices, local(): lax.all_gather(cross_key_weight, 'dp', axis=0, tiled=True)  157 us
    all_gather x1, waiting for transfers between devices, local(): lax.all_gather(cross_value_weight, 'dp', axis=0, tiled=True)  154 us
    all_gather x1, waiting for transfers between devices, local(): lax.all_gather(velocity_weight, 'dp', axis=0, tiled=True)  153 us
    all_gather x1, waiting for transfers between devices, local(): lax.all_gather(cross_output_weight, 'dp', axis=1, tiled=True)  152 us
    all_gather x1, waiting for transfers between devices, local(): lax.all_gather(cross_query_weight, 'dp', axis=0, tiled=True)  150 us
    all_gather x1, waiting for transfers between devices, local(): lax.all_gather(input_weight, 'dp', axis=1, tiled=True)  103 us
  transfers between devices with their start and end apart: 11, of which 9 were waited for; matrix products, arithmetic and copies ran while one was open for 2% of the time, Pallas kernels for 0%

commit v1 on v0

v1 whole, which is shorter than its diff:
```python
import math
import types

import jax
import jax.numpy as jnp
import numpy as np
from jax import lax
from jax.experimental import pallas as pl
from jax.experimental.pallas import tpu as pltpu
from jax.sharding import PartitionSpec as P

F32 = jnp.float32
BF16 = jnp.bfloat16
MESH = pl.DeviceIdType.MESH
HIGHEST = lax.Precision.HIGHEST
EPSILON = 1e-06
STEPS = 1000
FRAMES = 360
PADDED = 384
SCALE = 1.0 / math.sqrt(128)

INPUTS = [
    "states", "cap_len", "step_index", "motion_len", "gain", "q_gain", "k_gain", "cosine", "sine",
    "eq", "ek", "ev", "eo", "clean", "noise", "w_in", "vel", "wq", "wk", "wv", "wo",
]
OUTPUTS = ["loss", "packed"]

BUFFERS = dict(
    w_qkv=((4096, 768), BF16),
    w_out=((512, 4096), BF16),
    c0=((32, 1, 384), F32),
    gx=((8, 64, 512), BF16),
    wkv=((16, 2, 64, 512), BF16),
    zsb=((32, 16, 256), BF16),
    zrb=((32, 16, 256), BF16),
    zsf=((32, 8, 256), F32),
    zrf=((32, 8, 256), F32),
    zst=((32, 1, 768), F32),
    zrt=((32, 1, 768), F32),
    agb=((32, 16, 256), BF16),
    agf=((2, 32, 8, 256), F32),
    ra_send=((4, 64, 512), BF16),
    ra_recv=((4, 64, 512), BF16),
    rb_send=((4, 64, 512), BF16),
    rb_recv=((4, 64, 512), BF16),
    r_own=((4, 64, 512), F32),
    cap_own=((64, 512), BF16),
    caps=((4, 2, 64, 512), BF16),
    kvx_send=((64, 512), BF16),
    kvx_recv=((64, 512), BF16),
    blend=((PADDED, 256), BF16),
    query=((PADDED, 256), BF16),
    hid_v=((PADDED, 256), F32),
    va_send=((4, 48, 256), BF16),
    va_recv=((4, 48, 256), BF16),
    v_own=((4, 48, 256), F32),
    vb_send=((4, 48, 256), BF16),
    vb_recv=((4, 48, 256), BF16),
    vg=((8, 48, 256), BF16),
    dkx=((2, 2, 64, 256), BF16),
    dk=((4, 2, 64, 256), BF16),
    dv=((4, 2, 64, 256), BF16),
    cap_k=((4, 2, 64, 512), BF16),
    cap_v=((4, 4, 2, 64, 128), BF16),
    gk_send=((4, 128, 256), BF16),
    gk_recv=((4, 128, 256), BF16),
    gv_send=((4, 128, 256), BF16),
    gv_recv=((4, 128, 256), BF16),
    hs=((32, 16, 256), BF16),
    hr=((32, 16, 256), BF16),
    hp=((32, 1, 384), F32),
    hg=((32, 16, 256), BF16),
)

SEMAPHORES = dict(
    load=4,
    c0_s=1, c0_r=1,
    gx_s=8, gx_r=8,
    wkv_s=32, wkv_r=(16, 2),
    zb_s=1, zb_r=1, zf_s=1, zf_r=1, zt_s=1, zt_r=1,
    ab_s=1, ab_r=1, af_s=1, af_r=1, ap_s=1, ap_r=1,
    ra_s=4, ra_r=4, rb_s=4, rb_r=4,
    cp_s=8, cp_r=(4, 2),
    kvx_s=1, kvx_r=1,
    va_s=1, va_r=1, vb_s=4, vb_r=4, vg_s=8, vg_r=8,
    dx_s=2, dx_r=2, dk_s=4, dk_r=4, dv_s=4, dv_r=4,
    ck_s=4, ck_r=4, cv_s=4, cv_r=4,
    gk_s=4, gk_r=4, gv_s=4, gv_r=4,
    hs_s=1, hs_r=1, hp_s=1, hp_r=1, hg_s=1, hg_r=1,
)


def dot(a, b, left, right, precision=None):
    return lax.dot_general(
        a, b, (((left,), (right,)), ((), ())), precision=precision, preferred_element_type=F32
    )


def nn(a, b, precision=None):
    return dot(a, b, 1, 0, precision)


def nt(a, b, precision=None):
    return dot(a, b, 1, 1, precision)


def tn(a, b, precision=None):
    return dot(a, b, 0, 0, precision)


def softmax(scores):
    top = jnp.max(scores, axis=-1, keepdims=True)
    weights = jnp.exp(scores - top)
    return weights / jnp.sum(weights, axis=-1, keepdims=True)


def remote(source, target, send, receive, dp, tensor):
    return pltpu.make_async_remote_copy(
        src_ref=source,
        dst_ref=target,
        send_sem=send,
        recv_sem=receive,
        device_id=(dp, tensor),
        device_id_type=MESH,
    )


def kernel(*refs):
    names = INPUTS + [n + "_out" for n in OUTPUTS] + list(BUFFERS) + list(SEMAPHORES)
    r = types.SimpleNamespace(**dict(zip(names, refs, strict=True)))

    d = lax.axis_index("dp")
    t = lax.axis_index("tensor")
    zl = lax.div(d, 16)
    xy = lax.rem(d, 16)
    x = lax.div(xy, 4)
    y = lax.rem(xy, 4)
    zh = lax.div(t, 2)
    c = lax.rem(t, 2)
    mate = t + 1 - 2 * c
    other = (1 - zl) * 16 + xy
    pending = []

    def start(copy):
        copy.start()
        pending.append(copy)

    def turn(base, k, size):
        return lax.rem(base + k, size)

    def plane(xx, yy):
        return zl * 16 + xx * 4 + yy

    def arrived(slot, semaphore):
        remote(slot, slot, semaphore, semaphore, other, t).wait_recv()

    def all_arrived(buffer, semaphore):
        most = buffer.at[pl.ds(0, 31)]
        remote(most, most, semaphore, semaphore, other, t).wait_recv()

    def all_left(buffer, semaphore):
        most = buffer.at[pl.ds(0, 31)]
        remote(most, most, semaphore, semaphore, other, t).wait_send()

    def over_dp(body):
        def step(k, carry):
            body(k, turn(d, k, 32))
            return carry

        lax.fori_loop(1, 32, step, 0)

    loads = [
        pltpu.make_async_copy(r.eq, r.w_qkv.at[:, pl.ds(0, 512)], r.load.at[0]),
        pltpu.make_async_copy(r.ek, r.w_qkv.at[:, pl.ds(512, 128)], r.load.at[1]),
        pltpu.make_async_copy(r.ev, r.w_qkv.at[:, pl.ds(640, 128)], r.load.at[2]),
        pltpu.make_async_copy(r.eo, r.w_out, r.load.at[3]),
    ]
    for load in loads:
        load.start()

    barrier = pltpu.get_barrier_semaphore()

    def signal(dp, tensor):
        pl.semaphore_signal(barrier, inc=1, device_id=(dp, tensor), device_id_type=MESH)

    over_dp(lambda k, peer: signal(peer, t))
    signal(d, mate)
    for k in (1, 2, 3):
        signal(d, turn(zh, k, 4) * 2 + c)
        signal(other, turn(zh, k, 4) * 2 + c)

    r.gx[t] = r.states[0]
    wk_v = r.wk[...]
    wv_v = r.wv[...]
    for half in (0, 1):
        r.wkv[xy, half, :, 0:256] = wk_v[64 * half : 64 * half + 64]
        r.wkv[xy, half, :, 256:512] = wv_v[64 * half : 64 * half + 64]
    w_in_v = r.w_in[...]
    w_in_t = w_in_v.astype(F32)
    decay = -math.log(10000.0) / 1024.0
    step_f = jnp.full((8, 128), r.step_index[0], jnp.int32).astype(F32)
    place = (
        lax.broadcasted_iota(jnp.int32, (8, 128), 0) * 128
        + lax.broadcasted_iota(jnp.int32, (8, 128), 1)
    ).astype(F32)
    all_angles = step_f * jnp.exp(decay * place)
    all_cos = jnp.cos(all_angles)
    all_sin = jnp.sin(all_angles)

    def total(tile):
        return jnp.sum(jnp.sum(tile, axis=1, keepdims=True), axis=0, keepdims=True)

    own_mean = total(all_cos + all_sin) / 2048.0
    time_square = total((all_cos - own_mean) ** 2 + (all_sin - own_mean) ** 2)
    lane = lax.broadcasted_iota(jnp.int32, (1, 128), 1)
    r.c0[d, :, 0:256] = jnp.sum(w_in_t, axis=0, keepdims=True)
    r.c0[d, :, 256:384] = jnp.where(lane == 0, step_f[0:1], own_mean)

    pl.semaphore_wait(barrier, 38)

    for k in (2, 1, 3):
        start(remote(r.gx.at[t], r.gx.at[t], r.gx_s.at[k], r.gx_r.at[t], d, turn(zh, k, 4) * 2 + c))
    start(remote(r.gx.at[t], r.gx.at[t], r.gx_s.at[0], r.gx_r.at[t], d, mate))

    def c0_copy(k, peer):
        return remote(r.c0.at[d], r.c0.at[d], r.c0_s.at[0], r.c0_r.at[0], peer, t)

    over_dp(lambda k, peer: c0_copy(k, peer).start())

    def wkv_send(slot, half, dp, index):
        ref = r.wkv.at[slot, half]
        start(remote(ref, ref, r.wkv_s.at[index], r.wkv_r.at[slot, half], dp, t))

    for k in (1, 3, 2):
        wkv_send(xy, 0, plane(turn(x, k, 4), y), k - 1)
        wkv_send(xy, 1, plane(x, turn(y, k, 4)), 2 + k)

    all_arrived(r.c0, r.c0_r.at[0])
    facts = r.c0[...].reshape(32, 384)
    w_mean = jnp.sum(facts[:, 0:256], axis=0, keepdims=True) / 2048.0
    steps = facts[:, 256:257]
    step_means = facts[:, 257:258]
    column = (
        lax.broadcasted_iota(jnp.int32, (1, 64), 1) + lax.rem(d, 16) * 64
    ).astype(F32)
    angles = steps * jnp.exp(decay * column)
    cos_part = jnp.full((32, 64), zl, jnp.int32) == 0
    times = jnp.where(cos_part, jnp.cos(angles), jnp.sin(angles))
    times_c = times - step_means
    w_c = w_in_t - w_mean
    vel_v = r.vel[...]
    wq_v = r.wq[...]
    part_a = tn(w_c.astype(BF16), wq_v).reshape(32, 8, 256)
    part_m = tn(r.wo[...], vel_v).reshape(32, 8, 256)
    r.zsb[...] = jnp.concatenate([part_a, part_m], axis=1).astype(BF16)
    first_core = jnp.full((256, 256), c, jnp.int32) == 0
    part_f = jnp.where(first_core, tn(w_in_v, vel_v), tn(w_c, w_c, HIGHEST))
    r.zsf[...] = part_f.reshape(32, 8, 256)
    time_rows = jnp.concatenate(
        [
            nn(times_c, wq_v.astype(F32), HIGHEST),
            nn(times, vel_v.astype(F32), HIGHEST),
            nn(times_c, w_c, HIGHEST),
        ],
        axis=1,
    )
    r.zst[...] = time_rows.reshape(32, 1, 768)
    r.zrb[d] = r.zsb[d]
    r.zrf[d] = r.zsf[d]
    r.zrt[d] = r.zst[d]

    def z_copies(k, peer):
        return (
            remote(r.zsb.at[peer], r.zrb.at[d], r.zb_s.at[0], r.zb_r.at[0], peer, t),
            remote(r.zsf.at[peer], r.zrf.at[d], r.zf_s.at[0], r.zf_r.at[0], peer, t),
            remote(r.zst.at[peer], r.zrt.at[d], r.zt_s.at[0], r.zt_r.at[0], peer, t),
        )

    def z_start(k, peer):
        for copy in z_copies(k, peer):
            copy.start()

    for load in loads[:3]:
        load.wait()

    def project(slot, sums, square):
        chunk = r.gx[slot].astype(F32)
        square = square + jnp.sum(chunk * chunk, axis=1, keepdims=True)
        row = pl.multiple_of(slot * 512, 512)
        scaled = (chunk * r.gain[slot]).astype(BF16)
        return sums + nn(scaled, r.w_qkv[pl.ds(row, 512), :]), square

    sums, square = project(t, jnp.zeros((64, 768), F32), jnp.zeros((64, 1), F32))
    for k in (1, 3, 2):
        slot = turn(zh, k, 4) * 2 + c
        arrived(r.gx.at[slot], r.gx_r.at[slot])
        start(remote(r.gx.at[slot], r.gx.at[slot], r.gx_s.at[4 + k], r.gx_r.at[slot], d, mate))
        sums, square = project(slot, sums, square)

    over_dp(z_start)

    arrived(r.gx.at[mate], r.gx_r.at[mate])
    sums, square = project(mate, sums, square)
    for k in (1, 3, 2):
        slot = turn(zh, k, 4) * 2 + (1 - c)
        arrived(r.gx.at[slot], r.gx_r.at[slot])
        sums, square = project(slot, sums, square)

    def wkv_second(first, k_list):
        for k in k_list:
            if k:
                slot = turn(x, k, 4) * 4 + y
                arrived(r.wkv.at[slot, 0], r.wkv_r.at[slot, 0])
                slot = x * 4 + turn(y, k, 4)
                arrived(r.wkv.at[slot, 1], r.wkv_r.at[slot, 1])
            for j in (1, 3, 2):
                wkv_send(turn(x, k, 4) * 4 + y, 0, plane(x, turn(y, j, 4)), first + 6 * k + j - 1)
                wkv_send(
                    x * 4 + turn(y, k, 4), 1, plane(turn(x, j, 4), y), first + 6 * k + 2 + j
                )

    wkv_second(6, (0, 1, 3, 2))

    length = r.cap_len[0]
    rms = lax.rsqrt(square / 4096.0 + EPSILON)
    sums = sums * rms
    cosine = r.cosine[...]
    sine = r.sine[...]

    def turned(vectors, scaling):
        mean = jnp.mean(vectors * vectors, axis=1, keepdims=True)
        vectors = vectors * lax.rsqrt(mean + EPSILON) * scaling
        return (vectors * cosine + pltpu.roll(vectors, 64, 1) * sine).astype(BF16)

    q_gain = r.q_gain[...]
    queries = jnp.concatenate(
        [turned(sums[:, 128 * h : 128 * h + 128], q_gain) for h in range(4)], axis=0
    )
    keys = turned(sums[:, 512:640], r.k_gain[...])
    values = sums[:, 640:768].astype(BF16)
    scores = nt(queries, keys) * SCALE
    row = lax.rem(lax.broadcasted_iota(jnp.int32, (256, 64), 0), 64)
    col = lax.broadcasted_iota(jnp.int32, (256, 64), 1)
    scores = jnp.where((col <= row) & (col < length), scores, -1e30)
    mixed = nn(softmax(scores).astype(BF16), values).astype(BF16)
    mixed = jnp.concatenate([mixed[64 * h : 64 * h + 64] for h in range(4)], axis=1)

    loads[3].wait()
    for k in (1, 3, 2, 0):
        slot = turn(zh, k, 4)
        column = pl.multiple_of((slot * 2 + 1 - c) * 512, 512)
        r.ra_send[slot] = nn(mixed, r.w_out[:, pl.ds(column, 512)]).astype(BF16)
        start(
            remote(
                r.ra_send.at[slot], r.ra_recv.at[slot], r.ra_s.at[k], r.ra_r.at[slot], d, mate
            )
        )
    for k in (1, 3, 2, 0):
        slot = turn(zh, k, 4)
        column = pl.multiple_of((slot * 2 + c) * 512, 512)
        r.r_own[slot] = nn(mixed, r.w_out[:, pl.ds(column, 512)])
    for k in (2, 1, 3):
        slot = turn(zh, k, 4)
        arrived(r.ra_recv.at[slot], r.ra_r.at[slot])
        r.rb_send[slot] = (r.r_own[slot] + r.ra_recv[slot].astype(F32)).astype(BF16)
        start(
            remote(
                r.rb_send.at[slot], r.rb_recv.at[zh], r.rb_s.at[k], r.rb_r.at[zh], d, slot * 2 + c
            )
        )

    all_arrived(r.zrb, r.zb_r.at[0])
    all_arrived(r.zrf, r.zf_r.at[0])
    all_arrived(r.zrt, r.zt_r.at[0])
    r.agb[d] = jnp.sum(r.zrb[...].astype(F32), axis=0).astype(BF16)
    r.agf[c, d] = jnp.sum(r.zrf[...], axis=0)
    time_own = jnp.sum(r.zrt[...], axis=0)

    def a_copies(k, peer):
        return (
            remote(r.agb.at[d], r.agb.at[d], r.ab_s.at[0], r.ab_r.at[0], peer, t),
            remote(r.agf.at[c, d], r.agf.at[c, d], r.af_s.at[0], r.af_r.at[0], peer, t),
        )

    def a_start(k, peer):
        for copy in a_copies(k, peer):
            copy.start()

    over_dp(a_start)

    slot = zh
    arrived(r.ra_recv.at[slot], r.ra_r.at[slot])
    own = r.r_own[slot] + r.ra_recv[slot].astype(F32)
    for k in (1, 3, 2):
        slot = turn(zh, k, 4)
        arrived(r.rb_recv.at[slot], r.rb_r.at[slot])
        own = own + r.rb_recv[slot].astype(F32)
    r.cap_own[...] = (r.states[0].astype(F32) + own).astype(BF16)

    target = lax.div(zh, 2)
    mine = lax.rem(t, 4)
    inside = target == zl

    def cap_copy(k):
        return remote(
            r.cap_own,
            r.caps.at[mine, zl],
            r.cp_s.at[k],
            r.cp_r.at[mine, zl],
            target * 16 + xy,
            turn(zh, k, 4) * 2 + c,
        )

    for k in (2, 1, 3):
        start(cap_copy(k))

    @pl.when(inside)
    def _():
        r.caps[mine, zl] = r.cap_own[...]

    @pl.when(jnp.logical_not(inside))
    def _():
        cap_copy(0).start()

    clean = r.clean[0].astype(F32)
    noise = r.noise[0].astype(F32)
    tau = jnp.full((1, 256), r.step_index[0], jnp.int32).astype(F32) / STEPS
    margin = jnp.zeros((PADDED - FRAMES, 256), F32)
    blend_f = jnp.concatenate([(1.0 - tau) * clean + tau * noise, margin], axis=0)
    r.blend[...] = blend_f.astype(BF16)
    blend = r.blend[...]
    blend_f = blend.astype(F32)
    all_arrived(r.agb, r.ab_r.at[0])
    all_arrived(r.agf.at[c], r.af_r.at[0])
    start(remote(r.agf.at[c], r.agf.at[c], r.ap_s.at[0], r.ap_r.at[0], d, mate))
    matrices = r.agb[...].astype(F32)
    mat_a = matrices[:, 0:8].reshape(256, 256).astype(BF16)
    mat_m = matrices[:, 8:16].reshape(256, 256).astype(BF16)
    arrived(r.agf.at[1 - c], r.ap_r.at[0])
    mat_b = r.agf[0].reshape(256, 256)
    mat_s = r.agf[1].reshape(256, 256)
    r.hid_v[...] = nn(blend_f, mat_b, HIGHEST) + time_own[:, 256:512]
    spread = (nn(blend_f, mat_s, HIGHEST) + 2.0 * time_own[:, 512:768]) * blend_f
    variance = (jnp.sum(spread, axis=1, keepdims=True) + time_square) / 2048.0
    rstd = lax.rsqrt(jnp.maximum(variance, 0.0) + EPSILON)
    r.query[...] = ((nn(blend, mat_a) + time_own[:, 0:256]) * rstd).astype(BF16)

    for k in (0, 1, 2, 3):
        for j in (1, 2, 3):
            slot = turn(x, k, 4) * 4 + turn(y, j, 4)
            arrived(r.wkv.at[slot, 0], r.wkv_r.at[slot, 0])
            slot = turn(x, j, 4) * 4 + turn(y, k, 4)
            arrived(r.wkv.at[slot, 1], r.wkv_r.at[slot, 1])

    forwards = []
    for z in (0, 1):
        for near in (0, 1):
            chunk = near * 2 + c
            ref = r.caps.at[chunk, z]
            own_slot = inside & (chunk == mine) & (z == zl)

            @pl.when(jnp.logical_not(own_slot))
            def _(ref=ref, chunk=chunk, z=z):
                arrived(ref, r.cp_r.at[chunk, z])

            start(remote(ref, ref, r.cp_s.at[4 + 2 * z + near], r.cp_r.at[chunk, z], d, mate))

    def project_caption(chunk):
        rows = r.caps[chunk].reshape(128, 512)
        weights = r.wkv[pl.ds(chunk * 4, 4)].reshape(512, 512)
        return nn(rows, weights)

    both = project_caption(c) + project_caption(2 + c)
    for near in (0, 1):
        for z in (0, 1):
            chunk = near * 2 + 1 - c
            arrived(r.caps.at[chunk, z], r.cp_r.at[chunk, z])
        both = both + project_caption(near * 2 + 1 - c)
    second = jnp.full((64, 512), zl, jnp.int32) == 1
    r.kvx_send[...] = jnp.where(second, both[0:64], both[64:128]).astype(BF16)
    start(remote(r.kvx_send, r.kvx_recv, r.kvx_s.at[0], r.kvx_r.at[0], other, t))

    r.cap_k[x] = r.caps[x]
    for q in range(4):
        column = pl.multiple_of(y * 128, 128)
        r.cap_v[y, q] = r.caps[q, :, :, pl.ds(column, 128)]
    for k in (1, 3, 2):
        xx = turn(x, k, 4)
        start(
            remote(r.caps.at[xx], r.cap_k.at[x], r.ck_s.at[k], r.ck_r.at[x], plane(xx, y), t)
        )
        yy = turn(y, k, 4)
        column = pl.multiple_of(yy * 128, 128)
        start(
            remote(
                r.caps.at[:, :, :, pl.ds(column, 128)],
                r.cap_v.at[y],
                r.cv_s.at[k],
                r.cv_r.at[y],
                plane(x, yy),
                t,
            )
        )

    kv_own = jnp.where(second, both[64:128], both[0:64])
    arrived(r.kvx_recv, r.kvx_r.at[0])
    kv = (kv_own + r.kvx_recv[...].astype(F32)).astype(BF16)

    query = r.query[...]
    allowed = lax.broadcasted_iota(jnp.int32, (PADDED, 64), 1) < length
    probs = []
    attended = []
    for h in (0, 1):
        span = slice(128 * h, 128 * h + 128)
        scores = nt(query[:, span], kv[:, span]) * SCALE
        prob = softmax(jnp.where(allowed, scores, -1e30))
        probs.append(prob)
        attended.append(nn(prob.astype(BF16), kv[:, 256 + 128 * h : 384 + 128 * h]).astype(BF16))
    attended = jnp.concatenate(attended, axis=1)
    branch = nn(attended, mat_m).reshape(8, 48, 256)

    first_half = jnp.full((48, 256), c, jnp.int32) == 0
    for q in range(4):
        r.va_send[q] = jnp.where(first_half, branch[2 * q + 1], branch[2 * q]).astype(BF16)
        r.v_own[q] = jnp.where(first_half, branch[2 * q], branch[2 * q + 1])
    start(remote(r.va_send, r.va_recv, r.va_s.at[0], r.va_r.at[0], d, mate))
    arrived(r.va_recv, r.va_r.at[0])
    for k in (2, 1, 3):
        slot = turn(zh, k, 4)
        r.vb_send[slot] = (r.v_own[slot] + r.va_recv[slot].astype(F32)).astype(BF16)
        start(
            remote(
                r.vb_send.at[slot], r.vb_recv.at[zh], r.vb_s.at[k], r.vb_r.at[zh], d, slot * 2 + c
            )
        )
    own = r.v_own[zh] + r.va_recv[zh].astype(F32)
    for k in (1, 3, 2):
        slot = turn(zh, k, 4)
        arrived(r.vb_recv.at[slot], r.vb_r.at[slot])
        own = own + r.vb_recv[slot].astype(F32)
    r.vg[t] = own.astype(BF16)
    for k in (2, 1, 3):
        start(remote(r.vg.at[t], r.vg.at[t], r.vg_s.at[k], r.vg_r.at[t], d, turn(zh, k, 4) * 2 + c))
    start(remote(r.vg.at[t], r.vg.at[t], r.vg_s.at[0], r.vg_r.at[t], d, mate))
    for k in (1, 3, 2):
        slot = turn(zh, k, 4) * 2 + c
        arrived(r.vg.at[slot], r.vg_r.at[slot])
        start(remote(r.vg.at[slot], r.vg.at[slot], r.vg_s.at[4 + k], r.vg_r.at[slot], d, mate))
    arrived(r.vg.at[mate], r.vg_r.at[mate])
    for k in (1, 3, 2):
        slot = turn(zh, k, 4) * 2 + 1 - c
        arrived(r.vg.at[slot], r.vg_r.at[slot])

    predicted = r.hid_v[...] + r.vg[...].astype(F32).reshape(PADDED, 256)
    residual = predicted - jnp.concatenate([noise - clean, margin], axis=0)
    frames = jnp.full((PADDED, 1), r.motion_len[0], jnp.int32)
    live = lax.broadcasted_iota(jnp.int32, (PADDED, 1), 0) < frames
    row_weight = jnp.where(live, 1.0 / frames.astype(F32), 0.0)
    weighted = residual * row_weight
    loss_part = total(residual * weighted)
    d_vel = (2.0 * weighted).astype(BF16)
    d_att = nt(d_vel, mat_m).astype(BF16)

    d_keys = []
    d_values = []
    d_queries = []
    for h in (0, 1):
        span = slice(128 * h, 128 * h + 128)
        d_head = d_att[:, span]
        d_prob = nt(d_head, kv[:, 256 + 128 * h : 384 + 128 * h])
        prob = probs[h]
        delta = jnp.sum(prob * d_prob, axis=1, keepdims=True)
        d_score = (prob * (d_prob - delta) * SCALE).astype(BF16)
        d_values.append(tn(prob.astype(BF16), d_head))
        d_keys.append(tn(d_score, query[:, span]))
        d_queries.append(nn(d_score, kv[:, span]))
    r.dkx[0, zl] = jnp.concatenate(d_keys, axis=1).astype(BF16)
    r.dkx[1, zl] = jnp.concatenate(d_values, axis=1).astype(BF16)
    for i in (0, 1):
        ref = r.dkx.at[i, zl]
        start(remote(ref, ref, r.dx_s.at[i], r.dx_r.at[i], other, t))
    d_query = jnp.concatenate(d_queries, axis=1).astype(BF16).astype(F32) * rstd
    d_query_b = d_query.astype(BF16)
    mat_h = tn(blend, d_query_b).reshape(32, 8, 256)
    mat_g = tn(attended, d_vel).reshape(32, 8, 256)
    r.hs[...] = jnp.concatenate([mat_h, mat_g], axis=1).astype(BF16)
    r.hr[d] = r.hs[d]
    r.hp[d, :, 0:256] = jnp.sum(d_query, axis=0, keepdims=True)
    r.hp[d, :, 256:384] = jnp.broadcast_to(loss_part, (1, 128))

    for i in (0, 1):
        arrived(r.dkx.at[i, 1 - zl], r.dx_r.at[i])
    r.dk[x] = r.dkx[0]
    r.dv[y] = r.dkx[1]
    for k in (1, 3, 2):
        start(
            remote(
                r.dk.at[x], r.dk.at[x], r.dk_s.at[k], r.dk_r.at[x], plane(turn(x, k, 4), y), t
            )
        )
        start(
            remote(
                r.dv.at[y], r.dv.at[y], r.dv_s.at[k], r.dv_r.at[y], plane(x, turn(y, k, 4)), t
            )
        )

    def h_copies(k, peer):
        return (
            remote(r.hs.at[peer], r.hr.at[d], r.hs_s.at[0], r.hs_r.at[0], peer, t),
            remote(r.hp.at[d], r.hp.at[d], r.hp_s.at[0], r.hp_r.at[0], peer, t),
        )

    def h_start(k, peer):
        for copy in h_copies(k, peer):
            copy.start()

    over_dp(h_start)

    for k in (1, 3, 2):
        slot = turn(x, k, 4)
        arrived(r.cap_k.at[slot], r.ck_r.at[slot])
        arrived(r.dk.at[slot], r.dk_r.at[slot])
        slot = turn(y, k, 4)
        arrived(r.cap_v.at[slot], r.cv_r.at[slot])
        arrived(r.dv.at[slot], r.dv_r.at[slot])
    all_k = r.dk[...].reshape(512, 256)
    grad_k = tn(r.cap_k[...].reshape(512, 512), all_k).reshape(4, 128, 256)
    for q in range(4):
        r.gk_send[q] = grad_k[q].astype(BF16)
    r.gk_recv[y] = r.gk_send[y]
    for k in (1, 3, 2):
        yy = turn(y, k, 4)
        start(
            remote(
                r.gk_send.at[yy], r.gk_recv.at[y], r.gk_s.at[k], r.gk_r.at[y], plane(x, yy), t
            )
        )
    all_v = r.dv[...].reshape(512, 256)
    for q in range(4):
        grad_v = tn(r.cap_v[:, q].reshape(512, 128), all_v)
        r.gv_send[q] = grad_v.astype(BF16)
    r.gv_recv[x] = r.gv_send[x]
    for k in (1, 3, 2):
        xx = turn(x, k, 4)
        start(
            remote(
                r.gv_send.at[xx], r.gv_recv.at[x], r.gv_s.at[k], r.gv_r.at[x], plane(xx, y), t
            )
        )

    all_arrived(r.hr, r.hs_r.at[0])
    r.hg[d] = jnp.sum(r.hr[...].astype(F32), axis=0).astype(BF16)

    def g_copy(k, peer):
        return remote(r.hg.at[d], r.hg.at[d], r.hg_s.at[0], r.hg_r.at[0], peer, t)

    over_dp(lambda k, peer: g_copy(k, peer).start())
    all_arrived(r.hp, r.hp_r.at[0])
    sums_p = r.hp[...].reshape(32, 384)
    r.loss_out[...] = jnp.sum(sums_p[:, 256:384], axis=0, keepdims=True) / 8192.0
    all_arrived(r.hg, r.hg_r.at[0])
    grads = r.hg[...].astype(F32)
    sum_h = grads[:, 0:8].reshape(256, 256)
    sum_g = grads[:, 8:16].reshape(256, 256).astype(BF16)
    r.packed_out[0:64] = nn(w_c, sum_h, HIGHEST) + tn(times_c, sums_p[:, 0:256], HIGHEST)
    r.packed_out[320:384] = nt(r.vel[...], sum_g)
    for k in (1, 3, 2):
        slot = turn(y, k, 4)
        arrived(r.gk_recv.at[slot], r.gk_r.at[slot])
        slot = turn(x, k, 4)
        arrived(r.gv_recv.at[slot], r.gv_r.at[slot])
    r.packed_out[64:192] = jnp.sum(r.gk_recv[...].astype(F32), axis=0)
    r.packed_out[192:320] = jnp.sum(r.gv_recv[...].astype(F32), axis=0)

    for copy in pending:
        copy.wait_send()

    @pl.when(jnp.logical_not(inside))
    def _():
        cap_copy(0).wait_send()

    all_left(r.c0, r.c0_s.at[0])
    all_left(r.zrb, r.zb_s.at[0])
    all_left(r.zrf, r.zf_s.at[0])
    all_left(r.zrt, r.zt_s.at[0])
    all_left(r.agb, r.ab_s.at[0])
    all_left(r.agf.at[c], r.af_s.at[0])
    all_left(r.hr, r.hs_s.at[0])
    all_left(r.hp, r.hp_s.at[0])
    all_left(r.hg, r.hg_s.at[0])


def unpack(loss, packed, loss_out, gq, gk, gv, go):
    loss_out[...] = loss[...]
    gq[...] = packed[0:64]
    gk[...] = packed[64:192]
    gv[...] = packed[192:320]
    go[...] = packed[320:384]


def rope_tables():
    inverse = 1000000.0 ** (-(np.arange(64, dtype=np.float32) * 2.0 / 128))
    angles = np.arange(64, dtype=np.float32)[:, None] * inverse[None, :].astype(np.float32)
    angles = np.concatenate([angles, angles], axis=1).astype(np.float32)
    sign = np.where(np.arange(128) < 64, -1.0, 1.0)[None, :]
    return np.cos(angles).astype(np.float32), (np.sin(angles) * sign).astype(np.float32)


def local(
    encoder_input_states,
    caption_lengths,
    encoder_input_gain,
    query_head_gain,
    key_head_gain,
    encoder_query_weight,
    encoder_key_weight,
    encoder_value_weight,
    encoder_output_weight,
    clean_motion,
    noise,
    timestep_index,
    motion_lengths,
    input_weight,
    velocity_weight,
    cross_query_weight,
    cross_key_weight,
    cross_value_weight,
    cross_output_weight,
):
    vmem = pl.BlockSpec(memory_space=pltpu.VMEM)
    hbm = pl.BlockSpec(memory_space=pl.ANY)
    smem = pl.BlockSpec(memory_space=pltpu.SMEM)
    spec = {name: vmem for name in INPUTS}
    for name in ("cap_len", "step_index", "motion_len"):
        spec[name] = smem
    for name in ("eq", "ek", "ev", "eo"):
        spec[name] = hbm
    cosine, sine = rope_tables()
    packed = pl.pallas_call(
        kernel,
        out_shape=[
            jax.ShapeDtypeStruct((1, 128), F32),
            jax.ShapeDtypeStruct((384, 256), F32),
        ],
        in_specs=[spec[name] for name in INPUTS],
        out_specs=[vmem] * 2,
        scratch_shapes=[pltpu.VMEM(shape, kind) for shape, kind in BUFFERS.values()]
        + [
            pltpu.SemaphoreType.DMA(shape if isinstance(shape, tuple) else (shape,))
            for shape in SEMAPHORES.values()
        ],
        compiler_params=pltpu.CompilerParams(
            collective_id=0, has_side_effects=True, vmem_limit_bytes=56 * 2**20
        ),
        name="motion_block",
    )(
        encoder_input_states,
        caption_lengths,
        timestep_index,
        motion_lengths,
        encoder_input_gain.reshape(8, 1, 512),
        query_head_gain.reshape(1, 128),
        key_head_gain.reshape(1, 128),
        jnp.asarray(cosine),
        jnp.asarray(sine),
        encoder_query_weight,
        encoder_key_weight,
        encoder_value_weight,
        encoder_output_weight,
        clean_motion,
        noise,
        input_weight.T,
        velocity_weight,
        cross_query_weight,
        cross_key_weight,
        cross_value_weight,
        cross_output_weight.T,
    )
    loss, gq, gk, gv, go = pl.pallas_call(
        unpack,
        out_shape=[
            jax.ShapeDtypeStruct((1, 128), F32),
            jax.ShapeDtypeStruct((64, 256), F32),
            jax.ShapeDtypeStruct((128, 256), F32),
            jax.ShapeDtypeStruct((128, 256), F32),
            jax.ShapeDtypeStruct((64, 256), F32),
        ],
        in_specs=[vmem] * 2,
        out_specs=[vmem] * 5,
        name="unpack",
    )(*packed)
    return (loss[0, 0], gq, gk, gv, go.T)


def solution(mesh):
    placed = (
        P("dp", None, "tensor"),
        P("dp"),
        P(),
        P(),
        P(),
        P(None, "tensor"),
        P(None, "tensor"),
        P(None, "tensor"),
        P("tensor", None),
        P("dp", None, None),
        P("dp", None, None),
        P("dp"),
        P("dp"),
        P(None, "dp"),
        P("dp", None),
        P("dp", "tensor"),
        P("dp", "tensor"),
        P("dp", "tensor"),
        P("tensor", "dp"),
    )
    return jax.shard_map(
        local,
        mesh=mesh,
        in_specs=placed,
        out_specs=(P(), P("dp", "tensor"), P("dp", "tensor"), P("dp", "tensor"), P("tensor", "dp")),
        check_vma=False,
    )
```

time: 1470 us -> 99.7 us (0.07); the launches traced: 1450 us -> 99.6 us
  waiting for transfers between devices: 1290 us -> 0 us
  Pallas kernels: 0 us -> 97 us
  blocking collectives: 90.9 us -> 0 us
  matrix products: 40.3 us -> 0 us
  between operations: 19.5 us -> 2.58 us
    all_gather x6 -> x0, waiting for transfers between devices: 869 us -> none  [the longest x1 157 us: local(): lax.all_gather(cross_key_weight, 'dp', axis=0, tiled=True)]
    reduce_scatter x3 -> x0, waiting for transfers between devices: 414 us -> none  [the longest x1 172 us: local(): lax.psum_scatter(contract_rows(flattened_rows, d_keyval_rows).astype(jnp....]
    pallas_call x0 -> x2, Pallas kernels: none -> 97 us  [the longest x1 95.2 us: local(): pl.pallas_call(kernel, out_shape=[jax.ShapeDtypeStruct((1, 128), F32), ja...]
    psum x1 -> x0, blocking collectives: 70.6 us -> none  [local(): lax.psum(loss_part, 'dp') / (total_number * lax.axis_size('dp') * channels)]
    dot_general x22 -> x0, matrix products: 40.1 us -> none  [the longest x3 9.55 us: contract_rows(): lax.dot_general(left, right, (((0,), (0,)), ((), ())), preferred_element_...]
    all_gather x1 -> x0, blocking collectives: 20.3 us -> none  [local(): lax.all_gather(encoder_input_states, 'tensor', axis=2, tiled=True)]
  transfers between devices with their start and end apart: 11 -> 0, of which waited for: 9 -> 0; matrix products, arithmetic and copies ran while one was open for 2% -> 0% of each run, Pallas kernels for 0% -> 0%
where the time goes in v1:
time: 99.7 us; the launch traced here: 99.6 us
  Pallas kernels  97 us (97%)
  between operations  2.58 us (3%)
    pallas_call x1, Pallas kernels, local(): pl.pallas_call(kernel, out_shape=[jax.ShapeDtypeStruct((1, 128), F32), ja...  95.2 us

profile of v1, /device:TPU:1, one launch (start us, length us, event | category | flops | bytes accessed | tf_op | source)
XLA Modules:
  0.0 99.6 jit_solution(17432825246010606312)
XLA Ops:
  2.6 95.2 %motion_block.1 = (f32[1,128]{1,0:T(1,128)}, f32[384,256]{1,0:T(8,128)}) custom-call(bf16[1,64,512]{2,1,0:T(8,128)(2,1)} %refs_0_.1, s32[1]{0:T(128)S(6)} %copy.26.refs_1_, s32[1]{0:T(128)S(6)} %copy.27.refs_2_, s32[1]{0:T(128)S(6)} %copy.28.refs_3_, f32[8,1,512]{2,1,0:T(1,128)} %bitcast.10, f32[1,128]{1,0:T(1,128)} %bitcast.11, f32[1,128]{1,0:T(1,128)} %bitcast.12, ...), custom_call_target="tpu_custom_call" | custom-call | tf_op jit(solution)/shard_map/motion_block/pallas_call | solution.py:739
  97.8 1.7 %unpack.1 = (f32[1,128]{1,0:T(1,128)}, f32[64,256]{1,0:T(8,128)}, f32[128,256]{1,0:T(8,128)}, f32[128,256]{1,0:T(8,128)}, f32[64,256]{1,0:T(8,128)}) custom-call(f32[1,128]{1,0:T(1,128)} %get-tuple-element.12.loss, f32[384,256]{1,0:T(8,128)} %get-tuple-element.13.packed), custom_call_target="tpu_custom_call" | custom-call | tf_op jit(solution)/shard_map/unpack/pallas_call | solution.py:779

commit v2 on v1

--- a/solution.py
+++ b/solution.py
@@ -33,10 +33,8 @@
     wkv=((16, 2, 64, 512), BF16),
     zsb=((32, 16, 256), BF16),
     zrb=((32, 16, 256), BF16),
-    zsf=((32, 8, 256), F32),
-    zrf=((32, 8, 256), F32),
-    zst=((32, 1, 768), F32),
-    zrt=((32, 1, 768), F32),
+    zsf=((32, 8, 384), F32),
+    zrf=((32, 8, 384), F32),
     agb=((32, 16, 256), BF16),
     agf=((2, 32, 8, 256), F32),
     ra_send=((4, 64, 512), BF16),
@@ -62,13 +60,17 @@
     dv=((4, 2, 64, 256), BF16),
     cap_k=((4, 2, 64, 512), BF16),
     cap_v=((4, 4, 2, 64, 128), BF16),
+    cap_kt=((512, 512), BF16),
+    cap_vt=((4, 128, 512), BF16),
+    blend_t=((256, PADDED), BF16),
+    att_t=((256, PADDED), BF16),
+    prob_t=((2, 64, PADDED), BF16),
     gk_send=((4, 128, 256), BF16),
     gk_recv=((4, 128, 256), BF16),
     gv_send=((4, 128, 256), BF16),
     gv_recv=((4, 128, 256), BF16),
-    hs=((32, 16, 256), BF16),
-    hr=((32, 16, 256), BF16),
-    hp=((32, 1, 384), F32),
+    hs=((32, 16, 384), BF16),
+    hr=((32, 16, 384), BF16),
     hg=((32, 16, 256), BF16),
 )
 
@@ -77,7 +79,7 @@
     c0_s=1, c0_r=1,
     gx_s=8, gx_r=8,
     wkv_s=32, wkv_r=(16, 2),
-    zb_s=1, zb_r=1, zf_s=1, zf_r=1, zt_s=1, zt_r=1,
+    zb_s=1, zb_r=1, zf_s=1, zf_r=1,
     ab_s=1, ab_r=1, af_s=1, af_r=1, ap_s=1, ap_r=1,
     ra_s=4, ra_r=4, rb_s=4, rb_r=4,
     cp_s=8, cp_r=(4, 2),
@@ -86,7 +88,7 @@
     dx_s=2, dx_r=2, dk_s=4, dk_r=4, dv_s=4, dv_r=4,
     ck_s=4, ck_r=4, cv_s=4, cv_r=4,
     gk_s=4, gk_r=4, gv_s=4, gv_r=4,
-    hs_s=1, hs_r=1, hp_s=1, hp_r=1, hg_s=1, hg_r=1,
+    hs_s=1, hs_r=1, hg_s=1, hg_r=1,
 )
 
 
@@ -216,17 +218,17 @@
     r.c0[d, :, 0:256] = jnp.sum(w_in_t, axis=0, keepdims=True)
     r.c0[d, :, 256:384] = jnp.where(lane == 0, step_f[0:1], own_mean)
 
+    vel_v = r.vel[...]
+    wq_v = r.wq[...]
+    part_m = tn(r.wo[...], vel_v).reshape(32, 8, 256)
+    part_b = tn(w_in_v, vel_v)
+
     pl.semaphore_wait(barrier, 38)
 
     for k in (2, 1, 3):
         start(remote(r.gx.at[t], r.gx.at[t], r.gx_s.at[k], r.gx_r.at[t], d, turn(zh, k, 4) * 2 + c))
     start(remote(r.gx.at[t], r.gx.at[t], r.gx_s.at[0], r.gx_r.at[t], d, mate))
 
-    def c0_copy(k, peer):
-        return remote(r.c0.at[d], r.c0.at[d], r.c0_s.at[0], r.c0_r.at[0], peer, t)
-
-    over_dp(lambda k, peer: c0_copy(k, peer).start())
-
     def wkv_send(slot, half, dp, index):
         ref = r.wkv.at[slot, half]
         start(remote(ref, ref, r.wkv_s.at[index], r.wkv_r.at[slot, half], dp, t))
@@ -234,6 +236,98 @@
     for k in (1, 3, 2):
         wkv_send(xy, 0, plane(turn(x, k, 4), y), k - 1)
         wkv_send(xy, 1, plane(x, turn(y, k, 4)), 2 + k)
+
+    def c0_copy(k, peer):
+        return remote(r.c0.at[d], r.c0.at[d], r.c0_s.at[0], r.c0_r.at[0], peer, t)
+
+    over_dp(lambda k, peer: c0_copy(k, peer).start())
+
+    def wkv_second(first, k_list):
+        for k in k_list:
+            if k:
+                slot = turn(x, k, 4) * 4 + y
+                arrived(r.wkv.at[slot, 0], r.wkv_r.at[slot, 0])
+                slot = x * 4 + turn(y, k, 4)
+                arrived(r.wkv.at[slot, 1], r.wkv_r.at[slot, 1])
+            for j in (1, 3, 2):
+                wkv_send(turn(x, k, 4) * 4 + y, 0, plane(x, turn(y, j, 4)), first + 6 * k + j - 1)
+                wkv_send(
+                    x * 4 + turn(y, k, 4), 1, plane(turn(x, j, 4), y), first + 6 * k + 2 + j
+                )
+
+    wkv_second(6, (0, 1, 3, 2))
+
+    for load in loads[:3]:
+        load.wait()
+
+    def project(slot, sums, square):
+        chunk = r.gx[slot].astype(F32)
+        square = square + jnp.sum(chunk * chunk, axis=1, keepdims=True)
+        row = pl.multiple_of(slot * 512, 512)
+        scaled = (chunk * r.gain[slot]).astype(BF16)
+        return sums + nn(scaled, r.w_qkv[pl.ds(row, 512), :]), square
+
+    sums, square = project(t, jnp.zeros((64, 768), F32), jnp.zeros((64, 1), F32))
+    for k in (1, 3, 2):
+        slot = turn(zh, k, 4) * 2 + c
+        arrived(r.gx.at[slot], r.gx_r.at[slot])
+        start(remote(r.gx.at[slot], r.gx.at[slot], r.gx_s.at[4 + k], r.gx_r.at[slot], d, mate))
+        sums, square = project(slot, sums, square)
+
+    arrived(r.gx.at[mate], r.gx_r.at[mate])
+    sums, square = project(mate, sums, square)
+    for k in (1, 3, 2):
+        slot = turn(zh, k, 4) * 2 + (1 - c)
+        arrived(r.gx.at[slot], r.gx_r.at[slot])
+        sums, square = project(slot, sums, square)
+
+    length = r.cap_len[0]
+    rms = lax.rsqrt(square / 4096.0 + EPSILON)
+    sums = sums * rms
+    cosine = r.cosine[...]
+    sine = r.sine[...]
+
+    def turned(vectors, scaling):
+        mean = jnp.mean(vectors * vectors, axis=1, keepdims=True)
+        vectors = vectors * lax.rsqrt(mean + EPSILON) * scaling
+        return (vectors * cosine + pltpu.roll(vectors, 64, 1) * sine).astype(BF16)
+
+    q_gain = r.q_gain[...]
+    queries = jnp.concatenate(
+        [turned(sums[:, 128 * h : 128 * h + 128], q_gain) for h in range(4)], axis=0
+    )
+    keys = turned(sums[:, 512:640], r.k_gain[...])
+    values = sums[:, 640:768].astype(BF16)
+    scores = nt(queries, keys) * SCALE
+    row = lax.rem(lax.broadcasted_iota(jnp.int32, (256, 64), 0), 64)
+    col = lax.broadcasted_iota(jnp.int32, (256, 64), 1)
+    scores = jnp.where((col <= row) & (col < length), scores, -1e30)
+    mixed = nn(softmax(scores).astype(BF16), values).astype(BF16)
+    mixed = jnp.concatenate([mixed[64 * h : 64 * h + 64] for h in range(4)], axis=1)
+
+    loads[3].wait()
+    for k in (1, 3, 2, 0):
+        slot = turn(zh, k, 4)
+        column = pl.multiple_of((slot * 2 + 1 - c) * 512, 512)
+        r.ra_send[slot] = nn(mixed, r.w_out[:, pl.ds(column, 512)]).astype(BF16)
+        start(
+            remote(
+                r.ra_send.at[slot], r.ra_recv.at[slot], r.ra_s.at[k], r.ra_r.at[slot], d, mate
+            )
+        )
+    for k in (1, 3, 2, 0):
+        slot = turn(zh, k, 4)
+        column = pl.multiple_of((slot * 2 + c) * 512, 512)
+        r.r_own[slot] = nn(mixed, r.w_out[:, pl.ds(column, 512)])
+    for k in (2, 1, 3):
+        slot = turn(zh, k, 4)
+        arrived(r.ra_recv.at[slot], r.ra_r.at[slot])
+        r.rb_send[slot] = (r.r_own[slot] + r.ra_recv[slot].astype(F32)).astype(BF16)
+        start(
+            remote(
+                r.rb_send.at[slot], r.rb_recv.at[zh], r.rb_s.at[k], r.rb_r.at[zh], d, slot * 2 + c
+            )
+        )
 
     all_arrived(r.c0, r.c0_r.at[0])
     facts = r.c0[...].reshape(32, 384)
@@ -248,14 +342,11 @@
     times = jnp.where(cos_part, jnp.cos(angles), jnp.sin(angles))
     times_c = times - step_means
     w_c = w_in_t - w_mean
-    vel_v = r.vel[...]
-    wq_v = r.wq[...]
     part_a = tn(w_c.astype(BF16), wq_v).reshape(32, 8, 256)
-    part_m = tn(r.wo[...], vel_v).reshape(32, 8, 256)
     r.zsb[...] = jnp.concatenate([part_a, part_m], axis=1).astype(BF16)
     first_core = jnp.full((256, 256), c, jnp.int32) == 0
-    part_f = jnp.where(first_core, tn(w_in_v, vel_v), tn(w_c, w_c, HIGHEST))
-    r.zsf[...] = part_f.reshape(32, 8, 256)
+    part_f = jnp.where(first_core, part_b, tn(w_c, w_c, HIGHEST))
+    r.zsf[:, :, 0:256] = part_f.reshape(32, 8, 256)
     time_rows = jnp.concatenate(
         [
             nn(times_c, wq_v.astype(F32), HIGHEST),
@@ -264,129 +355,23 @@
         ],
         axis=1,
     )
-    r.zst[...] = time_rows.reshape(32, 1, 768)
+    for i in range(8):
+        part = time_rows[:, 128 * i : 128 * i + 128] if i < 6 else jnp.zeros((32, 128), F32)
+        r.zsf[:, i, 256:384] = part
     r.zrb[d] = r.zsb[d]
     r.zrf[d] = r.zsf[d]
-    r.zrt[d] = r.zst[d]
 
     def z_copies(k, peer):
         return (
             remote(r.zsb.at[peer], r.zrb.at[d], r.zb_s.at[0], r.zb_r.at[0], peer, t),
             remote(r.zsf.at[peer], r.zrf.at[d], r.zf_s.at[0], r.zf_r.at[0], peer, t),
-            remote(r.zst.at[peer], r.zrt.at[d], r.zt_s.at[0], r.zt_r.at[0], peer, t),
         )
 
     def z_start(k, peer):
         for copy in z_copies(k, peer):
             copy.start()
 
-    for load in loads[:3]:
-        load.wait()
-
-    def project(slot, sums, square):
-        chunk = r.gx[slot].astype(F32)
-        square = square + jnp.sum(chunk * chunk, axis=1, keepdims=True)
-        row = pl.multiple_of(slot * 512, 512)
-        scaled = (chunk * r.gain[slot]).astype(BF16)
-        return sums + nn(scaled, r.w_qkv[pl.ds(row, 512), :]), square
-
-    sums, square = project(t, jnp.zeros((64, 768), F32), jnp.zeros((64, 1), F32))
-    for k in (1, 3, 2):
-        slot = turn(zh, k, 4) * 2 + c
-        arrived(r.gx.at[slot], r.gx_r.at[slot])
-        start(remote(r.gx.at[slot], r.gx.at[slot], r.gx_s.at[4 + k], r.gx_r.at[slot], d, mate))
-        sums, square = project(slot, sums, square)
-
     over_dp(z_start)
-
-    arrived(r.gx.at[mate], r.gx_r.at[mate])
-    sums, square = project(mate, sums, square)
-    for k in (1, 3, 2):
-        slot = turn(zh, k, 4) * 2 + (1 - c)
-        arrived(r.gx.at[slot], r.gx_r.at[slot])
-        sums, square = project(slot, sums, square)
-
-    def wkv_second(first, k_list):
-        for k in k_list:
-            if k:
-                slot = turn(x, k, 4) * 4 + y
-                arrived(r.wkv.at[slot, 0], r.wkv_r.at[slot, 0])
-                slot = x * 4 + turn(y, k, 4)
-                arrived(r.wkv.at[slot, 1], r.wkv_r.at[slot, 1])
-            for j in (1, 3, 2):
-                wkv_send(turn(x, k, 4) * 4 + y, 0, plane(x, turn(y, j, 4)), first + 6 * k + j - 1)
-                wkv_send(
-                    x * 4 + turn(y, k, 4), 1, plane(turn(x, j, 4), y), first + 6 * k + 2 + j
-                )
-
-    wkv_second(6, (0, 1, 3, 2))
-
-    length = r.cap_len[0]
-    rms = lax.rsqrt(square / 4096.0 + EPSILON)
-    sums = sums * rms
-    cosine = r.cosine[...]
-    sine = r.sine[...]
-
-    def turned(vectors, scaling):
-        mean = jnp.mean(vectors * vectors, axis=1, keepdims=True)
-        vectors = vectors * lax.rsqrt(mean + EPSILON) * scaling
-        return (vectors * cosine + pltpu.roll(vectors, 64, 1) * sine).astype(BF16)
-
-    q_gain = r.q_gain[...]
-    queries = jnp.concatenate(
-        [turned(sums[:, 128 * h : 128 * h + 128], q_gain) for h in range(4)], axis=0
-    )
-    keys = turned(sums[:, 512:640], r.k_gain[...])
-    values = sums[:, 640:768].astype(BF16)
-    scores = nt(queries, keys) * SCALE
-    row = lax.rem(lax.broadcasted_iota(jnp.int32, (256, 64), 0), 64)
-    col = lax.broadcasted_iota(jnp.int32, (256, 64), 1)
-    scores = jnp.where((col <= row) & (col < length), scores, -1e30)
-    mixed = nn(softmax(scores).astype(BF16), values).astype(BF16)
-    mixed = jnp.concatenate([mixed[64 * h : 64 * h + 64] for h in range(4)], axis=1)
-
-    loads[3].wait()
-    for k in (1, 3, 2, 0):
-        slot = turn(zh, k, 4)
-        column = pl.multiple_of((slot * 2 + 1 - c) * 512, 512)
-        r.ra_send[slot] = nn(mixed, r.w_out[:, pl.ds(column, 512)]).astype(BF16)
-        start(
-            remote(
-                r.ra_send.at[slot], r.ra_recv.at[slot], r.ra_s.at[k], r.ra_r.at[slot], d, mate
-            )
-        )
-    for k in (1, 3, 2, 0):
-        slot = turn(zh, k, 4)
-        column = pl.multiple_of((slot * 2 + c) * 512, 512)
-        r.r_own[slot] = nn(mixed, r.w_out[:, pl.ds(column, 512)])
-    for k in (2, 1, 3):
-        slot = turn(zh, k, 4)
-        arrived(r.ra_recv.at[slot], r.ra_r.at[slot])
-        r.rb_send[slot] = (r.r_own[slot] + r.ra_recv[slot].astype(F32)).astype(BF16)
-        start(
-            remote(
-                r.rb_send.at[slot], r.rb_recv.at[zh], r.rb_s.at[k], r.rb_r.at[zh], d, slot * 2 + c
-            )
-        )
-
-    all_arrived(r.zrb, r.zb_r.at[0])
-    all_arrived(r.zrf, r.zf_r.at[0])
-    all_arrived(r.zrt, r.zt_r.at[0])
-    r.agb[d] = jnp.sum(r.zrb[...].astype(F32), axis=0).astype(BF16)
-    r.agf[c, d] = jnp.sum(r.zrf[...], axis=0)
-    time_own = jnp.sum(r.zrt[...], axis=0)
-
-    def a_copies(k, peer):
-        return (
-            remote(r.agb.at[d], r.agb.at[d], r.ab_s.at[0], r.ab_r.at[0], peer, t),
-            remote(r.agf.at[c, d], r.agf.at[c, d], r.af_s.at[0], r.af_r.at[0], peer, t),
-        )
-
-    def a_start(k, peer):
-        for copy in a_copies(k, peer):
-            copy.start()
-
-    over_dp(a_start)
 
     slot = zh
     arrived(r.ra_recv.at[slot], r.ra_r.at[slot])
@@ -421,6 +406,82 @@
     @pl.when(jnp.logical_not(inside))
     def _():
         cap_copy(0).start()
+
+    all_arrived(r.zrb, r.zb_r.at[0])
+    all_arrived(r.zrf, r.zf_r.at[0])
+    r.agb[d] = jnp.sum(r.zrb[...].astype(F32), axis=0).astype(BF16)
+    slabs = jnp.sum(r.zrf[...], axis=0)
+    r.agf[c, d] = slabs[:, 0:256]
+    time_own = jnp.concatenate([slabs[i : i + 1, 256:384] for i in range(6)], axis=1)
+
+    def a_copies(k, peer):
+        return (
+            remote(r.agb.at[d], r.agb.at[d], r.ab_s.at[0], r.ab_r.at[0], peer, t),
+            remote(r.agf.at[c, d], r.agf.at[c, d], r.af_s.at[0], r.af_r.at[0], peer, t),
+        )
+
+    def a_start(k, peer):
+        for copy in a_copies(k, peer):
+            copy.start()
+
+    over_dp(a_start)
+
+    for k in (0, 1, 2, 3):
+        for j in (1, 2, 3):
+            slot = turn(x, k, 4) * 4 + turn(y, j, 4)
+            arrived(r.wkv.at[slot, 0], r.wkv_r.at[slot, 0])
+            slot = turn(x, j, 4) * 4 + turn(y, k, 4)
+            arrived(r.wkv.at[slot, 1], r.wkv_r.at[slot, 1])
+
+    forwards = []
+    for z in (0, 1):
+        for near in (0, 1):
+            chunk = near * 2 + c
+            ref = r.caps.at[chunk, z]
+            own_slot = inside & (chunk == mine) & (z == zl)
+
+            @pl.when(jnp.logical_not(own_slot))
+            def _(ref=ref, chunk=chunk, z=z):
+                arrived(ref, r.cp_r.at[chunk, z])
+
+            start(remote(ref, ref, r.cp_s.at[4 + 2 * z + near], r.cp_r.at[chunk, z], d, mate))
+
+    def project_caption(chunk):
+        rows = r.caps[chunk].reshape(128, 512)
+        weights = r.wkv[pl.ds(chunk * 4, 4)].reshape(512, 512)
+        return nn(rows, weights)
+
+    both = project_caption(c) + project_caption(2 + c)
+    for near in (0, 1):
+        for z in (0, 1):
+            chunk = near * 2 + 1 - c
+            arrived(r.caps.at[chunk, z], r.cp_r.at[chunk, z])
+        both = both + project_caption(near * 2 + 1 - c)
+    second = jnp.full((64, 512), zl, jnp.int32) == 1
+    r.kvx_send[...] = jnp.where(second, both[0:64], both[64:128]).astype(BF16)
+    start(remote(r.kvx_send, r.kvx_recv, r.kvx_s.at[0], r.kvx_r.at[0], other, t))
+
+    r.cap_k[x] = r.caps[x]
+    for q in range(4):
+        column = pl.multiple_of(y * 128, 128)
+        r.cap_v[y, q] = r.caps[q, :, :, pl.ds(column, 128)]
+    for k in (1, 3, 2):
+        xx = turn(x, k, 4)
+        start(
+            remote(r.caps.at[xx], r.cap_k.at[x], r.ck_s.at[k], r.ck_r.at[x], plane(xx, y), t)
+        )
+        yy = turn(y, k, 4)
+        column = pl.multiple_of(yy * 128, 128)
+        start(
+            remote(
+                r.caps.at[:, :, :, pl.ds(column, 128)],
+                r.cap_v.at[y],
+                r.cv_s.at[k],
+                r.cv_r.at[y],
+                plane(x, yy),
+                t,
+            )
+        )
 
     clean = r.clean[0].astype(F32)
     noise = r.noise[0].astype(F32)
@@ -445,63 +506,6 @@
     rstd = lax.rsqrt(jnp.maximum(variance, 0.0) + EPSILON)
     r.query[...] = ((nn(blend, mat_a) + time_own[:, 0:256]) * rstd).astype(BF16)
 
-    for k in (0, 1, 2, 3):
-        for j in (1, 2, 3):
-            slot = turn(x, k, 4) * 4 + turn(y, j, 4)
-            arrived(r.wkv.at[slot, 0], r.wkv_r.at[slot, 0])
-            slot = turn(x, j, 4) * 4 + turn(y, k, 4)
-            arrived(r.wkv.at[slot, 1], r.wkv_r.at[slot, 1])
-
-    forwards = []
-    for z in (0, 1):
-        for near in (0, 1):
-            chunk = near * 2 + c
-            ref = r.caps.at[chunk, z]
-            own_slot = inside & (chunk == mine) & (z == zl)
-
-            @pl.when(jnp.logical_not(own_slot))
-            def _(ref=ref, chunk=chunk, z=z):
-                arrived(ref, r.cp_r.at[chunk, z])
-
-            start(remote(ref, ref, r.cp_s.at[4 + 2 * z + near], r.cp_r.at[chunk, z], d, mate))
-
-    def project_caption(chunk):
-        rows = r.caps[chunk].reshape(128, 512)
-        weights = r.wkv[pl.ds(chunk * 4, 4)].reshape(512, 512)
-        return nn(rows, weights)
-
-    both = project_caption(c) + project_caption(2 + c)
-    for near in (0, 1):
-        for z in (0, 1):
-            chunk = near * 2 + 1 - c
-            arrived(r.caps.at[chunk, z], r.cp_r.at[chunk, z])
-        both = both + project_caption(near * 2 + 1 - c)
-    second = jnp.full((64, 512), zl, jnp.int32) == 1
-    r.kvx_send[...] = jnp.where(second, both[0:64], both[64:128]).astype(BF16)
-    start(remote(r.kvx_send, r.kvx_recv, r.kvx_s.at[0], r.kvx_r.at[0], other, t))
-
-    r.cap_k[x] = r.caps[x]
-    for q in range(4):
-        column = pl.multiple_of(y * 128, 128)
-        r.cap_v[y, q] = r.caps[q, :, :, pl.ds(column, 128)]
-    for k in (1, 3, 2):
-        xx = turn(x, k, 4)
-        start(
-            remote(r.caps.at[xx], r.cap_k.at[x], r.ck_s.at[k], r.ck_r.at[x], plane(xx, y), t)
-        )
-        yy = turn(y, k, 4)
-        column = pl.multiple_of(yy * 128, 128)
-        start(
-            remote(
-                r.caps.at[:, :, :, pl.ds(column, 128)],
-                r.cap_v.at[y],
-                r.cv_s.at[k],
-                r.cv_r.at[y],
-                plane(x, yy),
-                t,
-            )
-        )
-
     kv_own = jnp.where(second, both[64:128], both[0:64])
     arrived(r.kvx_recv, r.kvx_r.at[0])
     kv = (kv_own + r.kvx_recv[...].astype(F32)).astype(BF16)
@@ -524,6 +528,9 @@
         r.va_send[q] = jnp.where(first_half, branch[2 * q + 1], branch[2 * q]).astype(BF16)
         r.v_own[q] = jnp.where(first_half, branch[2 * q], branch[2 * q + 1])
     start(remote(r.va_send, r.va_recv, r.va_s.at[0], r.va_r.at[0], d, mate))
+    r.att_t[...] = attended.T
+    for h in (0, 1):
+        r.prob_t[h] = probs[h].astype(BF16).T
     arrived(r.va_recv, r.va_r.at[0])
     for k in (2, 1, 3):
         slot = turn(zh, k, 4)
@@ -533,6 +540,11 @@
                 r.vb_send.at[slot], r.vb_recv.at[zh], r.vb_s.at[k], r.vb_r.at[zh], d, slot * 2 + c
             )
         )
+    r.blend_t[...] = blend.T
+    for k in (1, 3, 2):
+        slot = turn(x, k, 4)
+        arrived(r.cap_k.at[slot], r.ck_r.at[slot])
+    r.cap_kt[...] = r.cap_k[...].reshape(512, 512).T
     own = r.v_own[zh] + r.va_recv[zh].astype(F32)
     for k in (1, 3, 2):
         slot = turn(zh, k, 4)
@@ -542,6 +554,11 @@
     for k in (2, 1, 3):
         start(remote(r.vg.at[t], r.vg.at[t], r.vg_s.at[k], r.vg_r.at[t], d, turn(zh, k, 4) * 2 + c))
     start(remote(r.vg.at[t], r.vg.at[t], r.vg_s.at[0], r.vg_r.at[t], d, mate))
+    for k in (1, 3, 2):
+        slot = turn(y, k, 4)
+        arrived(r.cap_v.at[slot], r.cv_r.at[slot])
+    for q in range(4):
+        r.cap_vt[q] = r.cap_v[:, q].reshape(512, 128).T
     for k in (1, 3, 2):
         slot = turn(zh, k, 4) * 2 + c
         arrived(r.vg.at[slot], r.vg_r.at[slot])
@@ -561,73 +578,89 @@
     d_vel = (2.0 * weighted).astype(BF16)
     d_att = nt(d_vel, mat_m).astype(BF16)
 
-    d_keys = []
-    d_values = []
-    d_queries = []
-    for h in (0, 1):
-        span = slice(128 * h, 128 * h + 128)
-        d_head = d_att[:, span]
-        d_prob = nt(d_head, kv[:, 256 + 128 * h : 384 + 128 * h])
-        prob = probs[h]
-        delta = jnp.sum(prob * d_prob, axis=1, keepdims=True)
-        d_score = (prob * (d_prob - delta) * SCALE).astype(BF16)
-        d_values.append(tn(prob.astype(BF16), d_head))
-        d_keys.append(tn(d_score, query[:, span]))
-        d_queries.append(nn(d_score, kv[:, span]))
-    r.dkx[0, zl] = jnp.concatenate(d_keys, axis=1).astype(BF16)
+    heads = [d_att[:, 128 * h : 128 * h + 128] for h in (0, 1)]
+    d_values = [nn(r.prob_t[h], heads[h]) for h in (0, 1)]
     r.dkx[1, zl] = jnp.concatenate(d_values, axis=1).astype(BF16)
-    for i in (0, 1):
+
+    def dx_start(i):
         ref = r.dkx.at[i, zl]
         start(remote(ref, ref, r.dx_s.at[i], r.dx_r.at[i], other, t))
+
+    dx_start(1)
+    d_scores = []
+    for h in (0, 1):
+        d_prob = nt(heads[h], kv[:, 256 + 128 * h : 384 + 128 * h])
+        delta = jnp.sum(probs[h] * d_prob, axis=1, keepdims=True)
+        d_scores.append((probs[h] * (d_prob - delta) * SCALE).astype(BF16))
+    d_keys = [tn(d_scores[h], query[:, 128 * h : 128 * h + 128]) for h in (0, 1)]
+    r.dkx[0, zl] = jnp.concatenate(d_keys, axis=1).astype(BF16)
+    dx_start(0)
+    d_queries = [nn(d_scores[h], kv[:, 128 * h : 128 * h + 128]) for h in (0, 1)]
     d_query = jnp.concatenate(d_queries, axis=1).astype(BF16).astype(F32) * rstd
-    d_query_b = d_query.astype(BF16)
-    mat_h = tn(blend, d_query_b).reshape(32, 8, 256)
-    mat_g = tn(attended, d_vel).reshape(32, 8, 256)
-    r.hs[...] = jnp.concatenate([mat_h, mat_g], axis=1).astype(BF16)
+    mat_h = nn(r.blend_t[...], d_query.astype(BF16)).reshape(32, 8, 256)
+    mat_g = nn(r.att_t[...], d_vel).reshape(32, 8, 256)
+    r.hs[:, :, 0:256] = jnp.concatenate([mat_h, mat_g], axis=1).astype(BF16)
+    frame_sum = jnp.sum(d_query, axis=0, keepdims=True)
+    loss_high = loss_part.astype(BF16).astype(F32)
+    which = lax.broadcasted_iota(jnp.int32, (16, 128), 0)
+    extra = jnp.where(which == 2, loss_high, loss_part - loss_high)
+    extra = jnp.where(which == 1, frame_sum[:, 128:256], extra)
+    extra = jnp.where(which == 0, frame_sum[:, 0:128], extra)
+    r.hs[:, :, 256:384] = jnp.broadcast_to(extra.astype(BF16)[None], (32, 16, 128))
     r.hr[d] = r.hs[d]
-    r.hp[d, :, 0:256] = jnp.sum(d_query, axis=0, keepdims=True)
-    r.hp[d, :, 256:384] = jnp.broadcast_to(loss_part, (1, 128))
-
-    for i in (0, 1):
-        arrived(r.dkx.at[i, 1 - zl], r.dx_r.at[i])
+
+    def h_copy(k, peer):
+        return remote(r.hs.at[peer], r.hr.at[d], r.hs_s.at[0], r.hs_r.at[0], peer, t)
+
+    over_dp(lambda k, peer: h_copy(k, peer).start())
+
+    arrived(r.dkx.at[1, 1 - zl], r.dx_r.at[1])
+    r.dv[y] = r.dkx[1]
+    for k in (1, 3, 2):
+        start(
+            remote(
+                r.dv.at[y], r.dv.at[y], r.dv_s.at[k], r.dv_r.at[y], plane(x, turn(y, k, 4)), t
+            )
+        )
+    arrived(r.dkx.at[0, 1 - zl], r.dx_r.at[0])
     r.dk[x] = r.dkx[0]
-    r.dv[y] = r.dkx[1]
     for k in (1, 3, 2):
         start(
             remote(
                 r.dk.at[x], r.dk.at[x], r.dk_s.at[k], r.dk_r.at[x], plane(turn(x, k, 4), y), t
             )
         )
+
+    all_arrived(r.hr, r.hs_r.at[0])
+    arrivals = r.hr[...].astype(F32)
+    r.hg[d] = jnp.sum(arrivals[:, :, 0:256], axis=0).astype(BF16)
+
+    def g_copy(k, peer):
+        return remote(r.hg.at[d], r.hg.at[d], r.hg_s.at[0], r.hg_r.at[0], peer, t)
+
+    over_dp(lambda k, peer: g_copy(k, peer).start())
+
+    for k in (1, 3, 2):
+        slot = turn(y, k, 4)
+        arrived(r.dv.at[slot], r.dv_r.at[slot])
+    all_v = r.dv[...].reshape(512, 256)
+    for q in range(4):
+        r.gv_send[q] = nn(r.cap_vt[q], all_v).astype(BF16)
+    for k in (1, 3, 2):
+        xx = turn(x, k, 4)
         start(
             remote(
-                r.dv.at[y], r.dv.at[y], r.dv_s.at[k], r.dv_r.at[y], plane(x, turn(y, k, 4)), t
+                r.gv_send.at[xx], r.gv_recv.at[x], r.gv_s.at[k], r.gv_r.at[x], plane(xx, y), t
             )
         )
-
-    def h_copies(k, peer):
-        return (
-            remote(r.hs.at[peer], r.hr.at[d], r.hs_s.at[0], r.hs_r.at[0], peer, t),
-            remote(r.hp.at[d], r.hp.at[d], r.hp_s.at[0], r.hp_r.at[0], peer, t),
-        )
-
-    def h_start(k, peer):
-        for copy in h_copies(k, peer):
-            copy.start()
-
-    over_dp(h_start)
-
+    r.gv_recv[x] = r.gv_send[x]
     for k in (1, 3, 2):
         slot = turn(x, k, 4)
-        arrived(r.cap_k.at[slot], r.ck_r.at[slot])
         arrived(r.dk.at[slot], r.dk_r.at[slot])
-        slot = turn(y, k, 4)
-        arrived(r.cap_v.at[slot], r.cv_r.at[slot])
-        arrived(r.dv.at[slot], r.dv_r.at[slot])
     all_k = r.dk[...].reshape(512, 256)
-    grad_k = tn(r.cap_k[...].reshape(512, 512), all_k).reshape(4, 128, 256)
+    grad_k = nn(r.cap_kt[...], all_k).reshape(4, 128, 256)
     for q in range(4):
         r.gk_send[q] = grad_k[q].astype(BF16)
-    r.gk_recv[y] = r.gk_send[y]
     for k in (1, 3, 2):
         yy = turn(y, k, 4)
         start(
@@ -635,34 +668,16 @@
                 r.gk_send.at[yy], r.gk_recv.at[y], r.gk_s.at[k], r.gk_r.at[y], plane(x, yy), t
             )
         )
-    all_v = r.dv[...].reshape(512, 256)
-    for q in range(4):
-        grad_v = tn(r.cap_v[:, q].reshape(512, 128), all_v)
-        r.gv_send[q] = grad_v.astype(BF16)
-    r.gv_recv[x] = r.gv_send[x]
-    for k in (1, 3, 2):
-        xx = turn(x, k, 4)
-        start(
-            remote(
-                r.gv_send.at[xx], r.gv_recv.at[x], r.gv_s.at[k], r.gv_r.at[x], plane(xx, y), t
-            )
-        )
-
-    all_arrived(r.hr, r.hs_r.at[0])
-    r.hg[d] = jnp.sum(r.hr[...].astype(F32), axis=0).astype(BF16)
-
-    def g_copy(k, peer):
-        return remote(r.hg.at[d], r.hg.at[d], r.hg_s.at[0], r.hg_r.at[0], peer, t)
-
-    over_dp(lambda k, peer: g_copy(k, peer).start())
-    all_arrived(r.hp, r.hp_r.at[0])
-    sums_p = r.hp[...].reshape(32, 384)
-    r.loss_out[...] = jnp.sum(sums_p[:, 256:384], axis=0, keepdims=True) / 8192.0
+    r.gk_recv[y] = r.gk_send[y]
+
+    sums_p = jnp.concatenate([arrivals[:, 0, 256:384], arrivals[:, 1, 256:384]], axis=1)
+    losses = arrivals[:, 2, 256:384] + arrivals[:, 3, 256:384]
+    r.loss_out[...] = jnp.sum(losses, axis=0, keepdims=True) / 8192.0
     all_arrived(r.hg, r.hg_r.at[0])
     grads = r.hg[...].astype(F32)
     sum_h = grads[:, 0:8].reshape(256, 256)
     sum_g = grads[:, 8:16].reshape(256, 256).astype(BF16)
-    r.packed_out[0:64] = nn(w_c, sum_h, HIGHEST) + tn(times_c, sums_p[:, 0:256], HIGHEST)
+    r.packed_out[0:64] = nn(w_c, sum_h, HIGHEST) + tn(times_c, sums_p, HIGHEST)
     r.packed_out[320:384] = nt(r.vel[...], sum_g)
     for k in (1, 3, 2):
         slot = turn(y, k, 4)
@@ -682,11 +697,9 @@
     all_left(r.c0, r.c0_s.at[0])
     all_left(r.zrb, r.zb_s.at[0])
     all_left(r.zrf, r.zf_s.at[0])
-    all_left(r.zrt, r.zt_s.at[0])
     all_left(r.agb, r.ab_s.at[0])
     all_left(r.agf.at[c], r.af_s.at[0])
     all_left(r.hr, r.hs_s.at[0])
-    all_left(r.hp, r.hp_s.at[0])
     all_left(r.hg, r.hg_s.at[0])
 
 

time: 99.7 us -> 93.6 us (0.939)
  Pallas kernels: 97 us -> 90.9 us
    pallas_call x1, Pallas kernels: 95.2 us -> 89.1 us  [local(): pl.pallas_call(kernel, out_shape=[jax.ShapeDtypeStruct((1, 128), F32), ja...]
where the time goes in v2:
time: 93.6 us; the launch traced here: 93.4 us
  Pallas kernels  90.9 us (97%)
  between operations  2.58 us (3%)
    pallas_call x1, Pallas kernels, local(): pl.pallas_call(kernel, out_shape=[jax.ShapeDtypeStruct((1, 128), F32), ja...  89.1 us

profile of v2, /device:TPU:1, one launch (start us, length us, event | category | flops | bytes accessed | tf_op | source)
XLA Modules:
  0.0 93.4 jit_solution(1298441723452559625)
XLA Ops:
  2.6 89.1 %motion_block.1 = (f32[1,128]{1,0:T(1,128)}, f32[384,256]{1,0:T(8,128)}) custom-call(bf16[1,64,512]{2,1,0:T(8,128)(2,1)} %refs_0_.1, s32[1]{0:T(128)S(6)} %copy.26.refs_1_, s32[1]{0:T(128)S(6)} %copy.27.refs_2_, s32[1]{0:T(128)S(6)} %copy.28.refs_3_, f32[8,1,512]{2,1,0:T(1,128)} %bitcast.10, f32[1,128]{1,0:T(1,128)} %bitcast.11, f32[1,128]{1,0:T(1,128)} %bitcast.12, ...), custom_call_target="tpu_custom_call" | custom-call | tf_op jit(solution)/shard_map/motion_block/pallas_call | solution.py:752
  91.7 1.7 %unpack.1 = (f32[1,128]{1,0:T(1,128)}, f32[64,256]{1,0:T(8,128)}, f32[128,256]{1,0:T(8,128)}, f32[128,256]{1,0:T(8,128)}, f32[64,256]{1,0:T(8,128)}) custom-call(f32[1,128]{1,0:T(1,128)} %get-tuple-element.12.loss, f32[384,256]{1,0:T(8,128)} %get-tuple-element.13.packed), custom_call_target="tpu_custom_call" | custom-call | tf_op jit(solution)/shard_map/unpack/pallas_call | solution.py:792

commit v3 on v2

--- a/solution.py
+++ b/solution.py
@@ -69,8 +69,10 @@
     gk_recv=((4, 128, 256), BF16),
     gv_send=((4, 128, 256), BF16),
     gv_recv=((4, 128, 256), BF16),
-    hs=((32, 16, 384), BF16),
-    hr=((32, 16, 384), BF16),
+    hs=((32, 16, 256), BF16),
+    hr=((32, 16, 256), BF16),
+    gs=((32, 16, 128), BF16),
+    gr=((32, 16, 128), BF16),
     hg=((32, 16, 256), BF16),
 )
 
@@ -88,7 +90,7 @@
     dx_s=2, dx_r=2, dk_s=4, dk_r=4, dv_s=4, dv_r=4,
     ck_s=4, ck_r=4, cv_s=4, cv_r=4,
     gk_s=4, gk_r=4, gv_s=4, gv_r=4,
-    hs_s=1, hs_r=1, hg_s=1, hg_r=1,
+    hs_s=1, hs_r=1, gs_s=1, gs_r=1, hg_s=1, hg_r=1,
 )
 
 
@@ -229,6 +231,11 @@
         start(remote(r.gx.at[t], r.gx.at[t], r.gx_s.at[k], r.gx_r.at[t], d, turn(zh, k, 4) * 2 + c))
     start(remote(r.gx.at[t], r.gx.at[t], r.gx_s.at[0], r.gx_r.at[t], d, mate))
 
+    def c0_copy(k, peer):
+        return remote(r.c0.at[d], r.c0.at[d], r.c0_s.at[0], r.c0_r.at[0], peer, t)
+
+    over_dp(lambda k, peer: c0_copy(k, peer).start())
+
     def wkv_send(slot, half, dp, index):
         ref = r.wkv.at[slot, half]
         start(remote(ref, ref, r.wkv_s.at[index], r.wkv_r.at[slot, half], dp, t))
@@ -236,26 +243,6 @@
     for k in (1, 3, 2):
         wkv_send(xy, 0, plane(turn(x, k, 4), y), k - 1)
         wkv_send(xy, 1, plane(x, turn(y, k, 4)), 2 + k)
-
-    def c0_copy(k, peer):
-        return remote(r.c0.at[d], r.c0.at[d], r.c0_s.at[0], r.c0_r.at[0], peer, t)
-
-    over_dp(lambda k, peer: c0_copy(k, peer).start())
-
-    def wkv_second(first, k_list):
-        for k in k_list:
-            if k:
-                slot = turn(x, k, 4) * 4 + y
-                arrived(r.wkv.at[slot, 0], r.wkv_r.at[slot, 0])
-                slot = x * 4 + turn(y, k, 4)
-                arrived(r.wkv.at[slot, 1], r.wkv_r.at[slot, 1])
-            for j in (1, 3, 2):
-                wkv_send(turn(x, k, 4) * 4 + y, 0, plane(x, turn(y, j, 4)), first + 6 * k + j - 1)
-                wkv_send(
-                    x * 4 + turn(y, k, 4), 1, plane(turn(x, j, 4), y), first + 6 * k + 2 + j
-                )
-
-    wkv_second(6, (0, 1, 3, 2))
 
     for load in loads[:3]:
         load.wait()
@@ -268,66 +255,6 @@
         return sums + nn(scaled, r.w_qkv[pl.ds(row, 512), :]), square
 
     sums, square = project(t, jnp.zeros((64, 768), F32), jnp.zeros((64, 1), F32))
-    for k in (1, 3, 2):
-        slot = turn(zh, k, 4) * 2 + c
-        arrived(r.gx.at[slot], r.gx_r.at[slot])
-        start(remote(r.gx.at[slot], r.gx.at[slot], r.gx_s.at[4 + k], r.gx_r.at[slot], d, mate))
-        sums, square = project(slot, sums, square)
-
-    arrived(r.gx.at[mate], r.gx_r.at[mate])
-    sums, square = project(mate, sums, square)
-    for k in (1, 3, 2):
-        slot = turn(zh, k, 4) * 2 + (1 - c)
-        arrived(r.gx.at[slot], r.gx_r.at[slot])
-        sums, square = project(slot, sums, square)
-
-    length = r.cap_len[0]
-    rms = lax.rsqrt(square / 4096.0 + EPSILON)
-    sums = sums * rms
-    cosine = r.cosine[...]
-    sine = r.sine[...]
-
-    def turned(vectors, scaling):
-        mean = jnp.mean(vectors * vectors, axis=1, keepdims=True)
-        vectors = vectors * lax.rsqrt(mean + EPSILON) * scaling
-        return (vectors * cosine + pltpu.roll(vectors, 64, 1) * sine).astype(BF16)
-
-    q_gain = r.q_gain[...]
-    queries = jnp.concatenate(
-        [turned(sums[:, 128 * h : 128 * h + 128], q_gain) for h in range(4)], axis=0
-    )
-    keys = turned(sums[:, 512:640], r.k_gain[...])
-    values = sums[:, 640:768].astype(BF16)
-    scores = nt(queries, keys) * SCALE
-    row = lax.rem(lax.broadcasted_iota(jnp.int32, (256, 64), 0), 64)
-    col = lax.broadcasted_iota(jnp.int32, (256, 64), 1)
-    scores = jnp.where((col <= row) & (col < length), scores, -1e30)
-    mixed = nn(softmax(scores).astype(BF16), values).astype(BF16)
-    mixed = jnp.concatenate([mixed[64 * h : 64 * h + 64] for h in range(4)], axis=1)
-
-    loads[3].wait()
-    for k in (1, 3, 2, 0):
-        slot = turn(zh, k, 4)
-        column = pl.multiple_of((slot * 2 + 1 - c) * 512, 512)
-        r.ra_send[slot] = nn(mixed, r.w_out[:, pl.ds(column, 512)]).astype(BF16)
-        start(
-            remote(
-                r.ra_send.at[slot], r.ra_recv.at[slot], r.ra_s.at[k], r.ra_r.at[slot], d, mate
-            )
-        )
-    for k in (1, 3, 2, 0):
-        slot = turn(zh, k, 4)
-        column = pl.multiple_of((slot * 2 + c) * 512, 512)
-        r.r_own[slot] = nn(mixed, r.w_out[:, pl.ds(column, 512)])
-    for k in (2, 1, 3):
-        slot = turn(zh, k, 4)
-        arrived(r.ra_recv.at[slot], r.ra_r.at[slot])
-        r.rb_send[slot] = (r.r_own[slot] + r.ra_recv[slot].astype(F32)).astype(BF16)
-        start(
-            remote(
-                r.rb_send.at[slot], r.rb_recv.at[zh], r.rb_s.at[k], r.rb_r.at[zh], d, slot * 2 + c
-            )
-        )
 
     all_arrived(r.c0, r.c0_r.at[0])
     facts = r.c0[...].reshape(32, 384)
@@ -338,8 +265,8 @@
         lax.broadcasted_iota(jnp.int32, (1, 64), 1) + lax.rem(d, 16) * 64
     ).astype(F32)
     angles = steps * jnp.exp(decay * column)
-    cos_part = jnp.full((32, 64), zl, jnp.int32) == 0
-    times = jnp.where(cos_part, jnp.cos(angles), jnp.sin(angles))
+    quarter = jnp.full((32, 64), zl, jnp.int32).astype(F32) * (math.pi / 2.0)
+    times = jnp.cos(angles - quarter)
     times_c = times - step_means
     w_c = w_in_t - w_mean
     part_a = tn(w_c.astype(BF16), wq_v).reshape(32, 8, 256)
@@ -371,7 +298,102 @@
         for copy in z_copies(k, peer):
             copy.start()
 
+    def wkv_second(first, k_list):
+        for k in k_list:
+            if k:
+                slot = turn(x, k, 4) * 4 + y
+                arrived(r.wkv.at[slot, 0], r.wkv_r.at[slot, 0])
+                slot = x * 4 + turn(y, k, 4)
+                arrived(r.wkv.at[slot, 1], r.wkv_r.at[slot, 1])
+            for j in (1, 3, 2):
+                wkv_send(turn(x, k, 4) * 4 + y, 0, plane(x, turn(y, j, 4)), first + 6 * k + j - 1)
+                wkv_send(
+                    x * 4 + turn(y, k, 4), 1, plane(turn(x, j, 4), y), first + 6 * k + 2 + j
+                )
+
+    wkv_second(6, (0, 1, 3, 2))
+
+    for k in (1, 3, 2):
+        slot = turn(zh, k, 4) * 2 + c
+        arrived(r.gx.at[slot], r.gx_r.at[slot])
+        start(remote(r.gx.at[slot], r.gx.at[slot], r.gx_s.at[4 + k], r.gx_r.at[slot], d, mate))
+        sums, square = project(slot, sums, square)
+
     over_dp(z_start)
+
+    arrived(r.gx.at[mate], r.gx_r.at[mate])
+    sums, square = project(mate, sums, square)
+    for k in (1, 3, 2):
+        slot = turn(zh, k, 4) * 2 + (1 - c)
+        arrived(r.gx.at[slot], r.gx_r.at[slot])
+        sums, square = project(slot, sums, square)
+
+    length = r.cap_len[0]
+    rms = lax.rsqrt(square / 4096.0 + EPSILON)
+    sums = sums * rms
+    cosine = r.cosine[...]
+    sine = r.sine[...]
+
+    def turned(vectors, scaling):
+        mean = jnp.mean(vectors * vectors, axis=1, keepdims=True)
+        vectors = vectors * lax.rsqrt(mean + EPSILON) * scaling
+        return (vectors * cosine + pltpu.roll(vectors, 64, 1) * sine).astype(BF16)
+
+    q_gain = r.q_gain[...]
+    queries = jnp.concatenate(
+        [turned(sums[:, 128 * h : 128 * h + 128], q_gain) for h in range(4)], axis=0
+    )
+    keys = turned(sums[:, 512:640], r.k_gain[...])
+    values = sums[:, 640:768].astype(BF16)
+    scores = nt(queries, keys) * SCALE
+    row = lax.rem(lax.broadcasted_iota(jnp.int32, (256, 64), 0), 64)
+    col = lax.broadcasted_iota(jnp.int32, (256, 64), 1)
+    scores = jnp.where((col <= row) & (col < length), scores, -1e30)
+    mixed = nn(softmax(scores).astype(BF16), values).astype(BF16)
+    mixed = jnp.concatenate([mixed[64 * h : 64 * h + 64] for h in range(4)], axis=1)
+
+    loads[3].wait()
+    for k in (1, 3, 2, 0):
+        slot = turn(zh, k, 4)
+        column = pl.multiple_of((slot * 2 + 1 - c) * 512, 512)
+        r.ra_send[slot] = nn(mixed, r.w_out[:, pl.ds(column, 512)]).astype(BF16)
+        start(
+            remote(
+                r.ra_send.at[slot], r.ra_recv.at[slot], r.ra_s.at[k], r.ra_r.at[slot], d, mate
+            )
+        )
+    for k in (1, 3, 2, 0):
+        slot = turn(zh, k, 4)
+        column = pl.multiple_of((slot * 2 + c) * 512, 512)
+        r.r_own[slot] = nn(mixed, r.w_out[:, pl.ds(column, 512)])
+    for k in (2, 1, 3):
+        slot = turn(zh, k, 4)
+        arrived(r.ra_recv.at[slot], r.ra_r.at[slot])
+        r.rb_send[slot] = (r.r_own[slot] + r.ra_recv[slot].astype(F32)).astype(BF16)
+        start(
+            remote(
+                r.rb_send.at[slot], r.rb_recv.at[zh], r.rb_s.at[k], r.rb_r.at[zh], d, slot * 2 + c
+            )
+        )
+
+    all_arrived(r.zrb, r.zb_r.at[0])
+    all_arrived(r.zrf, r.zf_r.at[0])
+    r.agb[d] = jnp.sum(r.zrb[...].astype(F32), axis=0).astype(BF16)
+    slabs = jnp.sum(r.zrf[...], axis=0)
+    r.agf[c, d] = slabs[:, 0:256]
+    time_own = jnp.concatenate([slabs[i : i + 1, 256:384] for i in range(6)], axis=1)
+
+    def a_copies(k, peer):
+        return (
+            remote(r.agb.at[d], r.agb.at[d], r.ab_s.at[0], r.ab_r.at[0], peer, t),
+            remote(r.agf.at[c, d], r.agf.at[c, d], r.af_s.at[0], r.af_r.at[0], peer, t),
+        )
+
+    def a_start(k, peer):
+        for copy in a_copies(k, peer):
+            copy.start()
+
+    over_dp(a_start)
 
     slot = zh
     arrived(r.ra_recv.at[slot], r.ra_r.at[slot])
@@ -406,25 +428,6 @@
     @pl.when(jnp.logical_not(inside))
     def _():
         cap_copy(0).start()
-
-    all_arrived(r.zrb, r.zb_r.at[0])
-    all_arrived(r.zrf, r.zf_r.at[0])
-    r.agb[d] = jnp.sum(r.zrb[...].astype(F32), axis=0).astype(BF16)
-    slabs = jnp.sum(r.zrf[...], axis=0)
-    r.agf[c, d] = slabs[:, 0:256]
-    time_own = jnp.concatenate([slabs[i : i + 1, 256:384] for i in range(6)], axis=1)
-
-    def a_copies(k, peer):
-        return (
-            remote(r.agb.at[d], r.agb.at[d], r.ab_s.at[0], r.ab_r.at[0], peer, t),
-            remote(r.agf.at[c, d], r.agf.at[c, d], r.af_s.at[0], r.af_r.at[0], peer, t),
-        )
-
-    def a_start(k, peer):
-        for copy in a_copies(k, peer):
-            copy.start()
-
-    over_dp(a_start)
 
     for k in (0, 1, 2, 3):
         for j in (1, 2, 3):
@@ -595,18 +598,45 @@
     d_keys = [tn(d_scores[h], query[:, 128 * h : 128 * h + 128]) for h in (0, 1)]
     r.dkx[0, zl] = jnp.concatenate(d_keys, axis=1).astype(BF16)
     dx_start(0)
+    mat_g = nn(r.att_t[...], d_vel).reshape(32, 8, 256)
+    halves = [mat_g[:, :, 0:128], mat_g[:, :, 128:256]]
+    r.gs[...] = jnp.concatenate(halves, axis=1).astype(BF16)
+    r.gr[d] = r.gs[d]
+
+    def gs_copy(k, peer):
+        return remote(r.gs.at[peer], r.gr.at[d], r.gs_s.at[0], r.gs_r.at[0], peer, t)
+
+    over_dp(lambda k, peer: gs_copy(k, peer).start())
+
+    arrived(r.dkx.at[1, 1 - zl], r.dx_r.at[1])
+    r.dv[y] = r.dkx[1]
+    for k in (1, 3, 2):
+        start(
+            remote(
+                r.dv.at[y], r.dv.at[y], r.dv_s.at[k], r.dv_r.at[y], plane(x, turn(y, k, 4)), t
+            )
+        )
     d_queries = [nn(d_scores[h], kv[:, 128 * h : 128 * h + 128]) for h in (0, 1)]
+    arrived(r.dkx.at[0, 1 - zl], r.dx_r.at[0])
+    r.dk[x] = r.dkx[0]
+    for k in (1, 3, 2):
+        start(
+            remote(
+                r.dk.at[x], r.dk.at[x], r.dk_s.at[k], r.dk_r.at[x], plane(turn(x, k, 4), y), t
+            )
+        )
+
     d_query = jnp.concatenate(d_queries, axis=1).astype(BF16).astype(F32) * rstd
     mat_h = nn(r.blend_t[...], d_query.astype(BF16)).reshape(32, 8, 256)
-    mat_g = nn(r.att_t[...], d_vel).reshape(32, 8, 256)
-    r.hs[:, :, 0:256] = jnp.concatenate([mat_h, mat_g], axis=1).astype(BF16)
+    halves = [mat_h[:, :, 0:128], mat_h[:, :, 128:256]]
+    r.hs[:, :, 0:128] = jnp.concatenate(halves, axis=1).astype(BF16)
     frame_sum = jnp.sum(d_query, axis=0, keepdims=True)
     loss_high = loss_part.astype(BF16).astype(F32)
     which = lax.broadcasted_iota(jnp.int32, (16, 128), 0)
     extra = jnp.where(which == 2, loss_high, loss_part - loss_high)
     extra = jnp.where(which == 1, frame_sum[:, 128:256], extra)
     extra = jnp.where(which == 0, frame_sum[:, 0:128], extra)
-    r.hs[:, :, 256:384] = jnp.broadcast_to(extra.astype(BF16)[None], (32, 16, 128))
+    r.hs[:, :, 128:256] = jnp.broadcast_to(extra.astype(BF16)[None], (32, 16, 128))
     r.hr[d] = r.hs[d]
 
     def h_copy(k, peer):
@@ -614,26 +644,11 @@
 
     over_dp(lambda k, peer: h_copy(k, peer).start())
 
-    arrived(r.dkx.at[1, 1 - zl], r.dx_r.at[1])
-    r.dv[y] = r.dkx[1]
-    for k in (1, 3, 2):
-        start(
-            remote(
-                r.dv.at[y], r.dv.at[y], r.dv_s.at[k], r.dv_r.at[y], plane(x, turn(y, k, 4)), t
-            )
-        )
-    arrived(r.dkx.at[0, 1 - zl], r.dx_r.at[0])
-    r.dk[x] = r.dkx[0]
-    for k in (1, 3, 2):
-        start(
-            remote(
-                r.dk.at[x], r.dk.at[x], r.dk_s.at[k], r.dk_r.at[x], plane(turn(x, k, 4), y), t
-            )
-        )
-
+    all_arrived(r.gr, r.gs_r.at[0])
+    r.hg[d, :, 128:256] = jnp.sum(r.gr[...].astype(F32), axis=0).astype(BF16)
     all_arrived(r.hr, r.hs_r.at[0])
     arrivals = r.hr[...].astype(F32)
-    r.hg[d] = jnp.sum(arrivals[:, :, 0:256], axis=0).astype(BF16)
+    r.hg[d, :, 0:128] = jnp.sum(arrivals[:, :, 0:128], axis=0).astype(BF16)
 
     def g_copy(k, peer):
         return remote(r.hg.at[d], r.hg.at[d], r.hg_s.at[0], r.hg_r.at[0], peer, t)
@@ -670,13 +685,19 @@
         )
     r.gk_recv[y] = r.gk_send[y]
 
-    sums_p = jnp.concatenate([arrivals[:, 0, 256:384], arrivals[:, 1, 256:384]], axis=1)
-    losses = arrivals[:, 2, 256:384] + arrivals[:, 3, 256:384]
+    sums_p = jnp.concatenate([arrivals[:, 0, 128:256], arrivals[:, 1, 128:256]], axis=1)
+    losses = arrivals[:, 2, 128:256] + arrivals[:, 3, 128:256]
     r.loss_out[...] = jnp.sum(losses, axis=0, keepdims=True) / 8192.0
     all_arrived(r.hg, r.hg_r.at[0])
     grads = r.hg[...].astype(F32)
-    sum_h = grads[:, 0:8].reshape(256, 256)
-    sum_g = grads[:, 8:16].reshape(256, 256).astype(BF16)
+
+    def matrix(slabs):
+        left = slabs[:, 0:8].reshape(256, 128)
+        right = slabs[:, 8:16].reshape(256, 128)
+        return jnp.concatenate([left, right], axis=1)
+
+    sum_h = matrix(grads[:, :, 0:128])
+    sum_g = matrix(grads[:, :, 128:256]).astype(BF16)
     r.packed_out[0:64] = nn(w_c, sum_h, HIGHEST) + tn(times_c, sums_p, HIGHEST)
     r.packed_out[320:384] = nt(r.vel[...], sum_g)
     for k in (1, 3, 2):
@@ -700,6 +721,7 @@
     all_left(r.agb, r.ab_s.at[0])
     all_left(r.agf.at[c], r.af_s.at[0])
     all_left(r.hr, r.hs_s.at[0])
+    all_left(r.gr, r.gs_s.at[0])
     all_left(r.hg, r.hg_s.at[0])
 
 

time: 93.6 us -> 104 us (1.11)
  Pallas kernels: 90.9 us -> 101 us
    pallas_call x1, Pallas kernels: 89.1 us -> 99.3 us  [local(): pl.pallas_call(kernel, out_shape=[jax.ShapeDtypeStruct((1, 128), F32), ja...]
where the time goes in v3:
time: 104 us
  Pallas kernels  101 us (97%)
  between operations  2.58 us (2%)
    pallas_call x1, Pallas kernels, local(): pl.pallas_call(kernel, out_shape=[jax.ShapeDtypeStruct((1, 128), F32), ja...  99.3 us

profile of v3, /device:TPU:1, one launch (start us, length us, event | category | flops | bytes accessed | tf_op | source)
XLA Modules:
  0.0 103.7 jit_solution(16295582756034751070)
XLA Ops:
  2.6 99.3 %motion_block.1 = (f32[1,128]{1,0:T(1,128)}, f32[384,256]{1,0:T(8,128)}) custom-call(bf16[1,64,512]{2,1,0:T(8,128)(2,1)} %refs_0_.1, s32[1]{0:T(128)S(6)} %copy.26.refs_1_, s32[1]{0:T(128)S(6)} %copy.27.refs_2_, s32[1]{0:T(128)S(6)} %copy.28.refs_3_, f32[8,1,512]{2,1,0:T(1,128)} %bitcast.10, f32[1,128]{1,0:T(1,128)} %bitcast.11, f32[1,128]{1,0:T(1,128)} %bitcast.12, ...), custom_call_target="tpu_custom_call" | custom-call | tf_op jit(solution)/shard_map/motion_block/pallas_call | solution.py:774
  101.9 1.7 %unpack.1 = (f32[1,128]{1,0:T(1,128)}, f32[64,256]{1,0:T(8,128)}, f32[128,256]{1,0:T(8,128)}, f32[128,256]{1,0:T(8,128)}, f32[64,256]{1,0:T(8,128)}) custom-call(f32[1,128]{1,0:T(1,128)} %get-tuple-element.12.loss, f32[384,256]{1,0:T(8,128)} %get-tuple-element.13.packed), custom_call_target="tpu_custom_call" | custom-call | tf_op jit(solution)/shard_map/unpack/pallas_call | solution.py:814

commit v4 on v3

--- a/solution.py
+++ b/solution.py
@@ -69,10 +69,8 @@
     gk_recv=((4, 128, 256), BF16),
     gv_send=((4, 128, 256), BF16),
     gv_recv=((4, 128, 256), BF16),
-    hs=((32, 16, 256), BF16),
-    hr=((32, 16, 256), BF16),
-    gs=((32, 16, 128), BF16),
-    gr=((32, 16, 128), BF16),
+    hs=((32, 16, 384), BF16),
+    hr=((32, 16, 384), BF16),
     hg=((32, 16, 256), BF16),
 )
 
@@ -90,7 +88,7 @@
     dx_s=2, dx_r=2, dk_s=4, dk_r=4, dv_s=4, dv_r=4,
     ck_s=4, ck_r=4, cv_s=4, cv_r=4,
     gk_s=4, gk_r=4, gv_s=4, gv_r=4,
-    hs_s=1, hs_r=1, gs_s=1, gs_r=1, hg_s=1, hg_r=1,
+    hs_s=1, hs_r=1, hg_s=1, hg_r=1,
 )
 
 
@@ -231,11 +229,6 @@
         start(remote(r.gx.at[t], r.gx.at[t], r.gx_s.at[k], r.gx_r.at[t], d, turn(zh, k, 4) * 2 + c))
     start(remote(r.gx.at[t], r.gx.at[t], r.gx_s.at[0], r.gx_r.at[t], d, mate))
 
-    def c0_copy(k, peer):
-        return remote(r.c0.at[d], r.c0.at[d], r.c0_s.at[0], r.c0_r.at[0], peer, t)
-
-    over_dp(lambda k, peer: c0_copy(k, peer).start())
-
     def wkv_send(slot, half, dp, index):
         ref = r.wkv.at[slot, half]
         start(remote(ref, ref, r.wkv_s.at[index], r.wkv_r.at[slot, half], dp, t))
@@ -243,6 +236,26 @@
     for k in (1, 3, 2):
         wkv_send(xy, 0, plane(turn(x, k, 4), y), k - 1)
         wkv_send(xy, 1, plane(x, turn(y, k, 4)), 2 + k)
+
+    def c0_copy(k, peer):
+        return remote(r.c0.at[d], r.c0.at[d], r.c0_s.at[0], r.c0_r.at[0], peer, t)
+
+    over_dp(lambda k, peer: c0_copy(k, peer).start())
+
+    def wkv_second(first, k_list):
+        for k in k_list:
+            if k:
+                slot = turn(x, k, 4) * 4 + y
+                arrived(r.wkv.at[slot, 0], r.wkv_r.at[slot, 0])
+                slot = x * 4 + turn(y, k, 4)
+                arrived(r.wkv.at[slot, 1], r.wkv_r.at[slot, 1])
+            for j in (1, 3, 2):
+                wkv_send(turn(x, k, 4) * 4 + y, 0, plane(x, turn(y, j, 4)), first + 6 * k + j - 1)
+                wkv_send(
+                    x * 4 + turn(y, k, 4), 1, plane(turn(x, j, 4), y), first + 6 * k + 2 + j
+                )
+
+    wkv_second(6, (0, 1, 3, 2))
 
     for load in loads[:3]:
         load.wait()
@@ -298,21 +311,6 @@
         for copy in z_copies(k, peer):
             copy.start()
 
-    def wkv_second(first, k_list):
-        for k in k_list:
-            if k:
-                slot = turn(x, k, 4) * 4 + y
-                arrived(r.wkv.at[slot, 0], r.wkv_r.at[slot, 0])
-                slot = x * 4 + turn(y, k, 4)
-                arrived(r.wkv.at[slot, 1], r.wkv_r.at[slot, 1])
-            for j in (1, 3, 2):
-                wkv_send(turn(x, k, 4) * 4 + y, 0, plane(x, turn(y, j, 4)), first + 6 * k + j - 1)
-                wkv_send(
-                    x * 4 + turn(y, k, 4), 1, plane(turn(x, j, 4), y), first + 6 * k + 2 + j
-                )
-
-    wkv_second(6, (0, 1, 3, 2))
-
     for k in (1, 3, 2):
         slot = turn(zh, k, 4) * 2 + c
         arrived(r.gx.at[slot], r.gx_r.at[slot])
@@ -376,25 +374,6 @@
             )
         )
 
-    all_arrived(r.zrb, r.zb_r.at[0])
-    all_arrived(r.zrf, r.zf_r.at[0])
-    r.agb[d] = jnp.sum(r.zrb[...].astype(F32), axis=0).astype(BF16)
-    slabs = jnp.sum(r.zrf[...], axis=0)
-    r.agf[c, d] = slabs[:, 0:256]
-    time_own = jnp.concatenate([slabs[i : i + 1, 256:384] for i in range(6)], axis=1)
-
-    def a_copies(k, peer):
-        return (
-            remote(r.agb.at[d], r.agb.at[d], r.ab_s.at[0], r.ab_r.at[0], peer, t),
-            remote(r.agf.at[c, d], r.agf.at[c, d], r.af_s.at[0], r.af_r.at[0], peer, t),
-        )
-
-    def a_start(k, peer):
-        for copy in a_copies(k, peer):
-            copy.start()
-
-    over_dp(a_start)
-
     slot = zh
     arrived(r.ra_recv.at[slot], r.ra_r.at[slot])
     own = r.r_own[slot] + r.ra_recv[slot].astype(F32)
@@ -428,6 +407,25 @@
     @pl.when(jnp.logical_not(inside))
     def _():
         cap_copy(0).start()
+
+    all_arrived(r.zrb, r.zb_r.at[0])
+    all_arrived(r.zrf, r.zf_r.at[0])
+    r.agb[d] = jnp.sum(r.zrb[...].astype(F32), axis=0).astype(BF16)
+    slabs = jnp.sum(r.zrf[...], axis=0)
+    r.agf[c, d] = slabs[:, 0:256]
+    time_own = jnp.concatenate([slabs[i : i + 1, 256:384] for i in range(6)], axis=1)
+
+    def a_copies(k, peer):
+        return (
+            remote(r.agb.at[d], r.agb.at[d], r.ab_s.at[0], r.ab_r.at[0], peer, t),
+            remote(r.agf.at[c, d], r.agf.at[c, d], r.af_s.at[0], r.af_r.at[0], peer, t),
+        )
+
+    def a_start(k, peer):
+        for copy in a_copies(k, peer):
+            copy.start()
+
+    over_dp(a_start)
 
     for k in (0, 1, 2, 3):
         for j in (1, 2, 3):
@@ -599,15 +597,7 @@
     r.dkx[0, zl] = jnp.concatenate(d_keys, axis=1).astype(BF16)
     dx_start(0)
     mat_g = nn(r.att_t[...], d_vel).reshape(32, 8, 256)
-    halves = [mat_g[:, :, 0:128], mat_g[:, :, 128:256]]
-    r.gs[...] = jnp.concatenate(halves, axis=1).astype(BF16)
-    r.gr[d] = r.gs[d]
-
-    def gs_copy(k, peer):
-        return remote(r.gs.at[peer], r.gr.at[d], r.gs_s.at[0], r.gs_r.at[0], peer, t)
-
-    over_dp(lambda k, peer: gs_copy(k, peer).start())
-
+    d_queries = [nn(d_scores[h], kv[:, 128 * h : 128 * h + 128]) for h in (0, 1)]
     arrived(r.dkx.at[1, 1 - zl], r.dx_r.at[1])
     r.dv[y] = r.dkx[1]
     for k in (1, 3, 2):
@@ -616,7 +606,8 @@
                 r.dv.at[y], r.dv.at[y], r.dv_s.at[k], r.dv_r.at[y], plane(x, turn(y, k, 4)), t
             )
         )
-    d_queries = [nn(d_scores[h], kv[:, 128 * h : 128 * h + 128]) for h in (0, 1)]
+    d_query = jnp.concatenate(d_queries, axis=1).astype(BF16).astype(F32) * rstd
+    mat_h = nn(r.blend_t[...], d_query.astype(BF16)).reshape(32, 8, 256)
     arrived(r.dkx.at[0, 1 - zl], r.dx_r.at[0])
     r.dk[x] = r.dkx[0]
     for k in (1, 3, 2):
@@ -626,34 +617,20 @@
             )
         )
 
-    d_query = jnp.concatenate(d_queries, axis=1).astype(BF16).astype(F32) * rstd
-    mat_h = nn(r.blend_t[...], d_query.astype(BF16)).reshape(32, 8, 256)
-    halves = [mat_h[:, :, 0:128], mat_h[:, :, 128:256]]
-    r.hs[:, :, 0:128] = jnp.concatenate(halves, axis=1).astype(BF16)
+    r.hs[:, :, 0:256] = jnp.concatenate([mat_h, mat_g], axis=1).astype(BF16)
     frame_sum = jnp.sum(d_query, axis=0, keepdims=True)
     loss_high = loss_part.astype(BF16).astype(F32)
     which = lax.broadcasted_iota(jnp.int32, (16, 128), 0)
     extra = jnp.where(which == 2, loss_high, loss_part - loss_high)
     extra = jnp.where(which == 1, frame_sum[:, 128:256], extra)
     extra = jnp.where(which == 0, frame_sum[:, 0:128], extra)
-    r.hs[:, :, 128:256] = jnp.broadcast_to(extra.astype(BF16)[None], (32, 16, 128))
+    r.hs[:, :, 256:384] = jnp.broadcast_to(extra.astype(BF16)[None], (32, 16, 128))
     r.hr[d] = r.hs[d]
 
     def h_copy(k, peer):
         return remote(r.hs.at[peer], r.hr.at[d], r.hs_s.at[0], r.hs_r.at[0], peer, t)
 
     over_dp(lambda k, peer: h_copy(k, peer).start())
-
-    all_arrived(r.gr, r.gs_r.at[0])
-    r.hg[d, :, 128:256] = jnp.sum(r.gr[...].astype(F32), axis=0).astype(BF16)
-    all_arrived(r.hr, r.hs_r.at[0])
-    arrivals = r.hr[...].astype(F32)
-    r.hg[d, :, 0:128] = jnp.sum(arrivals[:, :, 0:128], axis=0).astype(BF16)
-
-    def g_copy(k, peer):
-        return remote(r.hg.at[d], r.hg.at[d], r.hg_s.at[0], r.hg_r.at[0], peer, t)
-
-    over_dp(lambda k, peer: g_copy(k, peer).start())
 
     for k in (1, 3, 2):
         slot = turn(y, k, 4)
@@ -685,21 +662,18 @@
         )
     r.gk_recv[y] = r.gk_send[y]
 
-    sums_p = jnp.concatenate([arrivals[:, 0, 128:256], arrivals[:, 1, 128:256]], axis=1)
-    losses = arrivals[:, 2, 128:256] + arrivals[:, 3, 128:256]
+    all_arrived(r.hr, r.hs_r.at[0])
+    arrivals = r.hr[...].astype(F32)
+    r.hg[d] = jnp.sum(arrivals[:, :, 0:256], axis=0).astype(BF16)
+
+    def g_copy(k, peer):
+        return remote(r.hg.at[d], r.hg.at[d], r.hg_s.at[0], r.hg_r.at[0], peer, t)
+
+    over_dp(lambda k, peer: g_copy(k, peer).start())
+
+    sums_p = jnp.concatenate([arrivals[:, 0, 256:384], arrivals[:, 1, 256:384]], axis=1)
+    losses = arrivals[:, 2, 256:384] + arrivals[:, 3, 256:384]
     r.loss_out[...] = jnp.sum(losses, axis=0, keepdims=True) / 8192.0
-    all_arrived(r.hg, r.hg_r.at[0])
-    grads = r.hg[...].astype(F32)
-
-    def matrix(slabs):
-        left = slabs[:, 0:8].reshape(256, 128)
-        right = slabs[:, 8:16].reshape(256, 128)
-        return jnp.concatenate([left, right], axis=1)
-
-    sum_h = matrix(grads[:, :, 0:128])
-    sum_g = matrix(grads[:, :, 128:256]).astype(BF16)
-    r.packed_out[0:64] = nn(w_c, sum_h, HIGHEST) + tn(times_c, sums_p, HIGHEST)
-    r.packed_out[320:384] = nt(r.vel[...], sum_g)
     for k in (1, 3, 2):
         slot = turn(y, k, 4)
         arrived(r.gk_recv.at[slot], r.gk_r.at[slot])
@@ -707,6 +681,12 @@
         arrived(r.gv_recv.at[slot], r.gv_r.at[slot])
     r.packed_out[64:192] = jnp.sum(r.gk_recv[...].astype(F32), axis=0)
     r.packed_out[192:320] = jnp.sum(r.gv_recv[...].astype(F32), axis=0)
+    all_arrived(r.hg, r.hg_r.at[0])
+    grads = r.hg[...].astype(F32)
+    sum_h = grads[:, 0:8].reshape(256, 256)
+    sum_g = grads[:, 8:16].reshape(256, 256).astype(BF16)
+    r.packed_out[0:64] = nn(w_c, sum_h, HIGHEST) + tn(times_c, sums_p, HIGHEST)
+    r.packed_out[320:384] = nt(r.vel[...], sum_g)
 
     for copy in pending:
         copy.wait_send()
@@ -721,7 +701,6 @@
     all_left(r.agb, r.ab_s.at[0])
     all_left(r.agf.at[c], r.af_s.at[0])
     all_left(r.hr, r.hs_s.at[0])
-    all_left(r.gr, r.gs_s.at[0])
     all_left(r.hg, r.hg_s.at[0])
 
 

time: 104 us -> 97 us (0.933)
  Pallas kernels: 101 us -> 94.3 us
    pallas_call x1, Pallas kernels: 99.3 us -> 92.5 us  [local(): pl.pallas_call(kernel, out_shape=[jax.ShapeDtypeStruct((1, 128), F32), ja...]
where the time goes in v4:
time: 97 us; the launch traced here: 96.8 us
  Pallas kernels  94.3 us (97%)
  between operations  2.58 us (3%)
    pallas_call x1, Pallas kernels, local(): pl.pallas_call(kernel, out_shape=[jax.ShapeDtypeStruct((1, 128), F32), ja...  92.5 us

profile of v4, /device:TPU:1, one launch (start us, length us, event | category | flops | bytes accessed | tf_op | source)
XLA Modules:
  0.0 96.8 jit_solution(15277177864437077484)
XLA Ops:
  2.6 92.5 %motion_block.1 = (f32[1,128]{1,0:T(1,128)}, f32[384,256]{1,0:T(8,128)}) custom-call(bf16[1,64,512]{2,1,0:T(8,128)(2,1)} %refs_0_.1, s32[1]{0:T(128)S(6)} %copy.26.refs_1_, s32[1]{0:T(128)S(6)} %copy.27.refs_2_, s32[1]{0:T(128)S(6)} %copy.28.refs_3_, f32[8,1,512]{2,1,0:T(1,128)} %bitcast.10, f32[1,128]{1,0:T(1,128)} %bitcast.11, f32[1,128]{1,0:T(1,128)} %bitcast.12, ...), custom_call_target="tpu_custom_call" | custom-call | tf_op jit(solution)/shard_map/motion_block/pallas_call | solution.py:753
  95.1 1.7 %unpack.1 = (f32[1,128]{1,0:T(1,128)}, f32[64,256]{1,0:T(8,128)}, f32[128,256]{1,0:T(8,128)}, f32[128,256]{1,0:T(8,128)}, f32[64,256]{1,0:T(8,128)}) custom-call(f32[1,128]{1,0:T(1,128)} %get-tuple-element.12.loss, f32[384,256]{1,0:T(8,128)} %get-tuple-element.13.packed), custom_call_target="tpu_custom_call" | custom-call | tf_op jit(solution)/shard_map/unpack/pallas_call | solution.py:793

commit v5 on v2

--- a/solution.py
+++ b/solution.py
@@ -31,12 +31,14 @@
     c0=((32, 1, 384), F32),
     gx=((8, 64, 512), BF16),
     wkv=((16, 2, 64, 512), BF16),
-    zsb=((32, 16, 256), BF16),
-    zrb=((32, 16, 256), BF16),
-    zsf=((32, 8, 384), F32),
-    zrf=((32, 8, 384), F32),
-    agb=((32, 16, 256), BF16),
-    agf=((2, 32, 8, 256), F32),
+    zsb=((16, 2, 16, 256), BF16),
+    zrb=((16, 2, 16, 256), BF16),
+    zsf=((16, 2, 8, 384), F32),
+    zrf=((16, 2, 8, 384), F32),
+    pzb=((2, 2, 16, 256), BF16),
+    pzf=((2, 2, 8, 384), F32),
+    agb=((16, 2, 16, 256), BF16),
+    agf=((2, 16, 2, 8, 256), F32),
     ra_send=((4, 64, 512), BF16),
     ra_recv=((4, 64, 512), BF16),
     rb_send=((4, 64, 512), BF16),
@@ -79,7 +81,7 @@
     c0_s=1, c0_r=1,
     gx_s=8, gx_r=8,
     wkv_s=32, wkv_r=(16, 2),
-    zb_s=1, zb_r=1, zf_s=1, zf_r=1,
+    zb_s=1, zb_r=1, zf_s=1, zf_r=1, pb_s=1, pb_r=1, pf_s=1, pf_r=1,
     ab_s=1, ab_r=1, af_s=1, af_r=1, ap_s=1, ap_r=1,
     ra_s=4, ra_r=4, rb_s=4, rb_r=4,
     cp_s=8, cp_r=(4, 2),
@@ -163,6 +165,21 @@
     def all_left(buffer, semaphore):
         most = buffer.at[pl.ds(0, 31)]
         remote(most, most, semaphore, semaphore, other, t).wait_send()
+
+    def plane_arrived(buffer, semaphore):
+        most = buffer.at[pl.ds(0, 15)]
+        remote(most, most, semaphore, semaphore, other, t).wait_recv()
+
+    def plane_left(buffer, semaphore):
+        most = buffer.at[pl.ds(0, 15)]
+        remote(most, most, semaphore, semaphore, other, t).wait_send()
+
+    def over_plane(body):
+        def step(k, carry):
+            body(turn(xy, k, 16))
+            return carry
+
+        lax.fori_loop(1, 16, step, 0)
 
     def over_dp(body):
         def step(k, carry):
@@ -268,11 +285,55 @@
         return sums + nn(scaled, r.w_qkv[pl.ds(row, 512), :]), square
 
     sums, square = project(t, jnp.zeros((64, 768), F32), jnp.zeros((64, 1), F32))
+
+    all_arrived(r.c0, r.c0_r.at[0])
+    facts = r.c0[...].reshape(32, 384)
+    w_mean = jnp.sum(facts[:, 0:256], axis=0, keepdims=True) / 2048.0
+    steps = facts[:, 256:257]
+    step_means = facts[:, 257:258]
+    column = (
+        lax.broadcasted_iota(jnp.int32, (1, 64), 1) + lax.rem(d, 16) * 64
+    ).astype(F32)
+    angles = steps * jnp.exp(decay * column)
+    quarter = jnp.full((32, 64), zl, jnp.int32).astype(F32) * (math.pi / 2.0)
+    times = jnp.cos(angles - quarter)
+    times_c = times - step_means
+    w_c = w_in_t - w_mean
+    part_a = tn(w_c.astype(BF16), wq_v).reshape(32, 8, 256)
+    slabs_b = jnp.concatenate([part_a, part_m], axis=1).astype(BF16)
+    first_core = jnp.full((256, 256), c, jnp.int32) == 0
+    part_f = jnp.where(first_core, part_b, tn(w_c, w_c, HIGHEST))
+    slabs_f = part_f.reshape(32, 8, 256)
+    time_rows = jnp.concatenate(
+        [
+            nn(times_c, wq_v.astype(F32), HIGHEST),
+            nn(times, vel_v.astype(F32), HIGHEST),
+            nn(times_c, w_c, HIGHEST),
+        ],
+        axis=1,
+    )
+    for z in (0, 1):
+        here = slice(16 * z, 16 * z + 16)
+        r.zsb[:, z] = slabs_b[here]
+        r.zsf[:, z, :, 0:256] = slabs_f[here]
+        for i in range(8):
+            part = time_rows[here, 128 * i : 128 * i + 128] if i < 6 else jnp.zeros((16, 128), F32)
+            r.zsf[:, z, i, 256:384] = part
+    r.zrb[xy] = r.zsb[xy]
+    r.zrf[xy] = r.zsf[xy]
+
+    def z_start(peer):
+        dp = zl * 16 + peer
+        remote(r.zsb.at[peer], r.zrb.at[xy], r.zb_s.at[0], r.zb_r.at[0], dp, t).start()
+        remote(r.zsf.at[peer], r.zrf.at[xy], r.zf_s.at[0], r.zf_r.at[0], dp, t).start()
+
     for k in (1, 3, 2):
         slot = turn(zh, k, 4) * 2 + c
         arrived(r.gx.at[slot], r.gx_r.at[slot])
         start(remote(r.gx.at[slot], r.gx.at[slot], r.gx_s.at[4 + k], r.gx_r.at[slot], d, mate))
         sums, square = project(slot, sums, square)
+
+    over_plane(z_start)
 
     arrived(r.gx.at[mate], r.gx_r.at[mate])
     sums, square = project(mate, sums, square)
@@ -329,50 +390,6 @@
             )
         )
 
-    all_arrived(r.c0, r.c0_r.at[0])
-    facts = r.c0[...].reshape(32, 384)
-    w_mean = jnp.sum(facts[:, 0:256], axis=0, keepdims=True) / 2048.0
-    steps = facts[:, 256:257]
-    step_means = facts[:, 257:258]
-    column = (
-        lax.broadcasted_iota(jnp.int32, (1, 64), 1) + lax.rem(d, 16) * 64
-    ).astype(F32)
-    angles = steps * jnp.exp(decay * column)
-    cos_part = jnp.full((32, 64), zl, jnp.int32) == 0
-    times = jnp.where(cos_part, jnp.cos(angles), jnp.sin(angles))
-    times_c = times - step_means
-    w_c = w_in_t - w_mean
-    part_a = tn(w_c.astype(BF16), wq_v).reshape(32, 8, 256)
-    r.zsb[...] = jnp.concatenate([part_a, part_m], axis=1).astype(BF16)
-    first_core = jnp.full((256, 256), c, jnp.int32) == 0
-    part_f = jnp.where(first_core, part_b, tn(w_c, w_c, HIGHEST))
-    r.zsf[:, :, 0:256] = part_f.reshape(32, 8, 256)
-    time_rows = jnp.concatenate(
-        [
-            nn(times_c, wq_v.astype(F32), HIGHEST),
-            nn(times, vel_v.astype(F32), HIGHEST),
-            nn(times_c, w_c, HIGHEST),
-        ],
-        axis=1,
-    )
-    for i in range(8):
-        part = time_rows[:, 128 * i : 128 * i + 128] if i < 6 else jnp.zeros((32, 128), F32)
-        r.zsf[:, i, 256:384] = part
-    r.zrb[d] = r.zsb[d]
-    r.zrf[d] = r.zsf[d]
-
-    def z_copies(k, peer):
-        return (
-            remote(r.zsb.at[peer], r.zrb.at[d], r.zb_s.at[0], r.zb_r.at[0], peer, t),
-            remote(r.zsf.at[peer], r.zrf.at[d], r.zf_s.at[0], r.zf_r.at[0], peer, t),
-        )
-
-    def z_start(k, peer):
-        for copy in z_copies(k, peer):
-            copy.start()
-
-    over_dp(z_start)
-
     slot = zh
     arrived(r.ra_recv.at[slot], r.ra_r.at[slot])
     own = r.r_own[slot] + r.ra_recv[slot].astype(F32)
@@ -407,24 +424,14 @@
     def _():
         cap_copy(0).start()
 
-    all_arrived(r.zrb, r.zb_r.at[0])
-    all_arrived(r.zrf, r.zf_r.at[0])
-    r.agb[d] = jnp.sum(r.zrb[...].astype(F32), axis=0).astype(BF16)
-    slabs = jnp.sum(r.zrf[...], axis=0)
-    r.agf[c, d] = slabs[:, 0:256]
-    time_own = jnp.concatenate([slabs[i : i + 1, 256:384] for i in range(6)], axis=1)
-
-    def a_copies(k, peer):
-        return (
-            remote(r.agb.at[d], r.agb.at[d], r.ab_s.at[0], r.ab_r.at[0], peer, t),
-            remote(r.agf.at[c, d], r.agf.at[c, d], r.af_s.at[0], r.af_r.at[0], peer, t),
-        )
-
-    def a_start(k, peer):
-        for copy in a_copies(k, peer):
-            copy.start()
-
-    over_dp(a_start)
+    plane_arrived(r.zrb, r.zb_r.at[0])
+    plane_arrived(r.zrf, r.zf_r.at[0])
+    plane_b = jnp.sum(r.zrb[...].astype(F32), axis=0)
+    plane_f = jnp.sum(r.zrf[...], axis=0)
+    r.pzb[zl] = plane_b.astype(BF16)
+    r.pzf[zl] = plane_f
+    start(remote(r.pzb.at[zl], r.pzb.at[zl], r.pb_s.at[0], r.pb_r.at[0], other, t))
+    start(remote(r.pzf.at[zl], r.pzf.at[zl], r.pf_s.at[0], r.pf_r.at[0], other, t))
 
     for k in (0, 1, 2, 3):
         for j in (1, 2, 3):
@@ -445,6 +452,22 @@
                 arrived(ref, r.cp_r.at[chunk, z])
 
             start(remote(ref, ref, r.cp_s.at[4 + 2 * z + near], r.cp_r.at[chunk, z], d, mate))
+
+    arrived(r.pzb.at[1 - zl], r.pb_r.at[0])
+    arrived(r.pzf.at[1 - zl], r.pf_r.at[0])
+    r.agb[xy] = (plane_b + r.pzb[1 - zl].astype(F32)).astype(BF16)
+    slabs = plane_f + r.pzf[1 - zl]
+    r.agf[c, xy] = slabs[:, :, 0:256]
+    late = jnp.full((8, 128), zl, jnp.int32) == 1
+    rows = jnp.where(late, slabs[1, :, 256:384], slabs[0, :, 256:384])
+    time_own = jnp.concatenate([rows[i : i + 1] for i in range(6)], axis=1)
+
+    def a_start(peer):
+        dp = zl * 16 + peer
+        remote(r.agb.at[xy], r.agb.at[xy], r.ab_s.at[0], r.ab_r.at[0], dp, t).start()
+        remote(r.agf.at[c, xy], r.agf.at[c, xy], r.af_s.at[0], r.af_r.at[0], dp, t).start()
+
+    over_plane(a_start)
 
     def project_caption(chunk):
         rows = r.caps[chunk].reshape(128, 512)
@@ -491,15 +514,19 @@
     r.blend[...] = blend_f.astype(BF16)
     blend = r.blend[...]
     blend_f = blend.astype(F32)
-    all_arrived(r.agb, r.ab_r.at[0])
-    all_arrived(r.agf.at[c], r.af_r.at[0])
+    plane_arrived(r.agb, r.ab_r.at[0])
+    plane_arrived(r.agf.at[c], r.af_r.at[0])
     start(remote(r.agf.at[c], r.agf.at[c], r.ap_s.at[0], r.ap_r.at[0], d, mate))
     matrices = r.agb[...].astype(F32)
-    mat_a = matrices[:, 0:8].reshape(256, 256).astype(BF16)
-    mat_m = matrices[:, 8:16].reshape(256, 256).astype(BF16)
+
+    def planes(slabs):
+        return jnp.concatenate([slabs[:, z].reshape(128, 256) for z in (0, 1)], axis=0)
+
+    mat_a = planes(matrices[:, :, 0:8]).astype(BF16)
+    mat_m = planes(matrices[:, :, 8:16]).astype(BF16)
     arrived(r.agf.at[1 - c], r.ap_r.at[0])
-    mat_b = r.agf[0].reshape(256, 256)
-    mat_s = r.agf[1].reshape(256, 256)
+    mat_b = planes(r.agf[0])
+    mat_s = planes(r.agf[1])
     r.hid_v[...] = nn(blend_f, mat_b, HIGHEST) + time_own[:, 256:512]
     spread = (nn(blend_f, mat_s, HIGHEST) + 2.0 * time_own[:, 512:768]) * blend_f
     variance = (jnp.sum(spread, axis=1, keepdims=True) + time_square) / 2048.0
@@ -695,10 +722,10 @@
         cap_copy(0).wait_send()
 
     all_left(r.c0, r.c0_s.at[0])
-    all_left(r.zrb, r.zb_s.at[0])
-    all_left(r.zrf, r.zf_s.at[0])
-    all_left(r.agb, r.ab_s.at[0])
-    all_left(r.agf.at[c], r.af_s.at[0])
+    plane_left(r.zrb, r.zb_s.at[0])
+    plane_left(r.zrf, r.zf_s.at[0])
+    plane_left(r.agb, r.ab_s.at[0])
+    plane_left(r.agf.at[c], r.af_s.at[0])
     all_left(r.hr, r.hs_s.at[0])
     all_left(r.hg, r.hg_s.at[0])
 

time: 93.6 us -> 96.5 us (1.031)
  Pallas kernels: 90.9 us -> 93.8 us
    pallas_call x1, Pallas kernels: 89.1 us -> 92.1 us  [local(): pl.pallas_call(kernel, out_shape=[jax.ShapeDtypeStruct((1, 128), F32), ja...]
where the time goes in v5:
time: 96.5 us; the launch traced here: 96.4 us
  Pallas kernels  93.8 us (97%)
  between operations  2.58 us (3%)
    pallas_call x1, Pallas kernels, local(): pl.pallas_call(kernel, out_shape=[jax.ShapeDtypeStruct((1, 128), F32), ja...  92.1 us

profile of v5, /device:TPU:1, one launch (start us, length us, event | category | flops | bytes accessed | tf_op | source)
XLA Modules:
  0.0 96.4 jit_solution(13117884141375167913)
XLA Ops:
  2.6 92.1 %motion_block.1 = (f32[1,128]{1,0:T(1,128)}, f32[384,256]{1,0:T(8,128)}) custom-call(bf16[1,64,512]{2,1,0:T(8,128)(2,1)} %refs_0_.1, s32[1]{0:T(128)S(6)} %copy.26.refs_1_, s32[1]{0:T(128)S(6)} %copy.27.refs_2_, s32[1]{0:T(128)S(6)} %copy.28.refs_3_, f32[8,1,512]{2,1,0:T(1,128)} %bitcast.10, f32[1,128]{1,0:T(1,128)} %bitcast.11, f32[1,128]{1,0:T(1,128)} %bitcast.12, ...), custom_call_target="tpu_custom_call" | custom-call | tf_op jit(solution)/shard_map/motion_block/pallas_call | solution.py:779
  94.6 1.7 %unpack.1 = (f32[1,128]{1,0:T(1,128)}, f32[64,256]{1,0:T(8,128)}, f32[128,256]{1,0:T(8,128)}, f32[128,256]{1,0:T(8,128)}, f32[64,256]{1,0:T(8,128)}) custom-call(f32[1,128]{1,0:T(1,128)} %get-tuple-element.12.loss, f32[384,256]{1,0:T(8,128)} %get-tuple-element.13.packed), custom_call_target="tpu_custom_call" | custom-call | tf_op jit(solution)/shard_map/unpack/pallas_call | solution.py:819

commit v6 on v5

--- a/solution.py
+++ b/solution.py
@@ -286,6 +286,67 @@
 
     sums, square = project(t, jnp.zeros((64, 768), F32), jnp.zeros((64, 1), F32))
 
+    for k in (1, 3, 2):
+        slot = turn(zh, k, 4) * 2 + c
+        arrived(r.gx.at[slot], r.gx_r.at[slot])
+        start(remote(r.gx.at[slot], r.gx.at[slot], r.gx_s.at[4 + k], r.gx_r.at[slot], d, mate))
+        sums, square = project(slot, sums, square)
+
+    arrived(r.gx.at[mate], r.gx_r.at[mate])
+    sums, square = project(mate, sums, square)
+    for k in (1, 3, 2):
+        slot = turn(zh, k, 4) * 2 + (1 - c)
+        arrived(r.gx.at[slot], r.gx_r.at[slot])
+        sums, square = project(slot, sums, square)
+
+    length = r.cap_len[0]
+    rms = lax.rsqrt(square / 4096.0 + EPSILON)
+    sums = sums * rms
+    cosine = r.cosine[...]
+    sine = r.sine[...]
+
+    def turned(vectors, scaling):
+        mean = jnp.mean(vectors * vectors, axis=1, keepdims=True)
+        vectors = vectors * lax.rsqrt(mean + EPSILON) * scaling
+        return (vectors * cosine + pltpu.roll(vectors, 64, 1) * sine).astype(BF16)
+
+    q_gain = r.q_gain[...]
+    queries = jnp.concatenate(
+        [turned(sums[:, 128 * h : 128 * h + 128], q_gain) for h in range(4)], axis=0
+    )
+    keys = turned(sums[:, 512:640], r.k_gain[...])
+    values = sums[:, 640:768].astype(BF16)
+    scores = nt(queries, keys) * SCALE
+    row = lax.rem(lax.broadcasted_iota(jnp.int32, (256, 64), 0), 64)
+    col = lax.broadcasted_iota(jnp.int32, (256, 64), 1)
+    scores = jnp.where((col <= row) & (col < length), scores, -1e30)
+    mixed = nn(softmax(scores).astype(BF16), values).astype(BF16)
+    mixed = jnp.concatenate([mixed[64 * h : 64 * h + 64] for h in range(4)], axis=1)
+
+    loads[3].wait()
+    for k in (1, 3, 2, 0):
+        slot = turn(zh, k, 4)
+        column = pl.multiple_of((slot * 2 + 1 - c) * 512, 512)
+        r.ra_send[slot] = nn(mixed, r.w_out[:, pl.ds(column, 512)]).astype(BF16)
+        start(
+            remote(
+                r.ra_send.at[slot], r.ra_recv.at[slot], r.ra_s.at[k], r.ra_r.at[slot], d, mate
+            )
+        )
+    for k in (1, 3, 2, 0):
+        slot = turn(zh, k, 4)
+        column = pl.multiple_of((slot * 2 + c) * 512, 512)
+        r.r_own[slot] = nn(mixed, r.w_out[:, pl.ds(column, 512)])
+    for k in (2, 1, 3):
+        slot = turn(zh, k, 4)
+        arrived(r.ra_recv.at[slot], r.ra_r.at[slot])
+        r.rb_send[slot] = (r.r_own[slot] + r.ra_recv[slot].astype(F32)).astype(BF16)
+        start(
+            remote(
+                r.rb_send.at[slot], r.rb_recv.at[zh], r.rb_s.at[k], r.rb_r.at[zh], d, slot * 2 + c
+            )
+        )
+
     all_arrived(r.c0, r.c0_r.at[0])
     facts = r.c0[...].reshape(32, 384)
     w_mean = jnp.sum(facts[:, 0:256], axis=0, keepdims=True) / 2048.0
@@ -327,68 +388,7 @@
         remote(r.zsb.at[peer], r.zrb.at[xy], r.zb_s.at[0], r.zb_r.at[0], dp, t).start()
         remote(r.zsf.at[peer], r.zrf.at[xy], r.zf_s.at[0], r.zf_r.at[0], dp, t).start()
 
-    for k in (1, 3, 2):
-        slot = turn(zh, k, 4) * 2 + c
-        arrived(r.gx.at[slot], r.gx_r.at[slot])
-        start(remote(r.gx.at[slot], r.gx.at[slot], r.gx_s.at[4 + k], r.gx_r.at[slot], d, mate))
-        sums, square = project(slot, sums, square)
-
     over_plane(z_start)
-
-    arrived(r.gx.at[mate], r.gx_r.at[mate])
-    sums, square = project(mate, sums, square)
-    for k in (1, 3, 2):
-        slot = turn(zh, k, 4) * 2 + (1 - c)
-        arrived(r.gx.at[slot], r.gx_r.at[slot])
-        sums, square = project(slot, sums, square)
-
-    length = r.cap_len[0]
-    rms = lax.rsqrt(square / 4096.0 + EPSILON)
-    sums = sums * rms
-    cosine = r.cosine[...]
-    sine = r.sine[...]
-
-    def turned(vectors, scaling):
-        mean = jnp.mean(vectors * vectors, axis=1, keepdims=True)
-        vectors = vectors * lax.rsqrt(mean + EPSILON) * scaling
-        return (vectors * cosine + pltpu.roll(vectors, 64, 1) * sine).astype(BF16)
-
-    q_gain = r.q_gain[...]
-    queries = jnp.concatenate(
-        [turned(sums[:, 128 * h : 128 * h + 128], q_gain) for h in range(4)], axis=0
-    )
-    keys = turned(sums[:, 512:640], r.k_gain[...])
-    values = sums[:, 640:768].astype(BF16)
-    scores = nt(queries, keys) * SCALE
-    row = lax.rem(lax.broadcasted_iota(jnp.int32, (256, 64), 0), 64)
-    col = lax.broadcasted_iota(jnp.int32, (256, 64), 1)
-    scores = jnp.where((col <= row) & (col < length), scores, -1e30)
-    mixed = nn(softmax(scores).astype(BF16), values).astype(BF16)
-    mixed = jnp.concatenate([mixed[64 * h : 64 * h + 64] for h in range(4)], axis=1)
-
-    loads[3].wait()
-    for k in (1, 3, 2, 0):
-        slot = turn(zh, k, 4)
-        column = pl.multiple_of((slot * 2 + 1 - c) * 512, 512)
-        r.ra_send[slot] = nn(mixed, r.w_out[:, pl.ds(column, 512)]).astype(BF16)
-        start(
-            remote(
-                r.ra_send.at[slot], r.ra_recv.at[slot], r.ra_s.at[k], r.ra_r.at[slot], d, mate
-            )
-        )
-    for k in (1, 3, 2, 0):
-        slot = turn(zh, k, 4)
-        column = pl.multiple_of((slot * 2 + c) * 512, 512)
-        r.r_own[slot] = nn(mixed, r.w_out[:, pl.ds(column, 512)])
-    for k in (2, 1, 3):
-        slot = turn(zh, k, 4)
-        arrived(r.ra_recv.at[slot], r.ra_r.at[slot])
-        r.rb_send[slot] = (r.r_own[slot] + r.ra_recv[slot].astype(F32)).astype(BF16)
-        start(
-            remote(
-                r.rb_send.at[slot], r.rb_recv.at[zh], r.rb_s.at[k], r.rb_r.at[zh], d, slot * 2 + c
-            )
-        )
 
     slot = zh
     arrived(r.ra_recv.at[slot], r.ra_r.at[slot])

time: 96.5 us -> 92 us (0.953)
  Pallas kernels: 93.8 us -> 89.3 us
    pallas_call x1, Pallas kernels: 92.1 us -> 87.5 us  [local(): pl.pallas_call(kernel, out_shape=[jax.ShapeDtypeStruct((1, 128), F32), ja...]
where the time goes in v6:
time: 92 us; the launch traced here: 91.8 us
  Pallas kernels  89.3 us (97%)
  between operations  2.58 us (3%)
    pallas_call x1, Pallas kernels, local(): pl.pallas_call(kernel, out_shape=[jax.ShapeDtypeStruct((1, 128), F32), ja...  87.5 us

profile of v6, /device:TPU:1, one launch (start us, length us, event | category | flops | bytes accessed | tf_op | source)
XLA Modules:
  0.0 91.8 jit_solution(1190360818562497563)
XLA Ops:
  2.6 87.5 %motion_block.1 = (f32[1,128]{1,0:T(1,128)}, f32[384,256]{1,0:T(8,128)}) custom-call(bf16[1,64,512]{2,1,0:T(8,128)(2,1)} %refs_0_.1, s32[1]{0:T(128)S(6)} %copy.26.refs_1_, s32[1]{0:T(128)S(6)} %copy.27.refs_2_, s32[1]{0:T(128)S(6)} %copy.28.refs_3_, f32[8,1,512]{2,1,0:T(1,128)} %bitcast.10, f32[1,128]{1,0:T(1,128)} %bitcast.11, f32[1,128]{1,0:T(1,128)} %bitcast.12, ...), custom_call_target="tpu_custom_call" | custom-call | tf_op jit(solution)/shard_map/motion_block/pallas_call | solution.py:779
  90.1 1.7 %unpack.1 = (f32[1,128]{1,0:T(1,128)}, f32[64,256]{1,0:T(8,128)}, f32[128,256]{1,0:T(8,128)}, f32[128,256]{1,0:T(8,128)}, f32[64,256]{1,0:T(8,128)}) custom-call(f32[1,128]{1,0:T(1,128)} %get-tuple-element.12.loss, f32[384,256]{1,0:T(8,128)} %get-tuple-element.13.packed), custom_call_target="tpu_custom_call" | custom-call | tf_op jit(solution)/shard_map/unpack/pallas_call | solution.py:819

commit v7 on v6

--- a/solution.py
+++ b/solution.py
@@ -79,7 +79,7 @@
 SEMAPHORES = dict(
     load=4,
     c0_s=1, c0_r=1,
-    gx_s=8, gx_r=8,
+    gx_s=12, gx_r=(8, 2),
     wkv_s=32, wkv_r=(16, 2),
     zb_s=1, zb_r=1, zf_s=1, zf_r=1, pb_s=1, pb_r=1, pf_s=1, pf_r=1,
     ab_s=1, ab_r=1, af_s=1, af_r=1, ap_s=1, ap_r=1,
@@ -242,9 +242,22 @@
 
     pl.semaphore_wait(barrier, 38)
 
-    for k in (2, 1, 3):
-        start(remote(r.gx.at[t], r.gx.at[t], r.gx_s.at[k], r.gx_r.at[t], d, turn(zh, k, 4) * 2 + c))
-    start(remote(r.gx.at[t], r.gx.at[t], r.gx_s.at[0], r.gx_r.at[t], d, mate))
+    def gx_half(slot, half):
+        return r.gx.at[slot, pl.ds(32 * half, 32)]
+
+    def gx_send(slot, half, step, index):
+        ref = gx_half(slot, half)
+        peer = turn(zh, step, 4) * 2 + c
+        start(remote(ref, ref, r.gx_s.at[index], r.gx_r.at[slot, half], d, peer))
+
+    def gx_arrived(slot, half):
+        arrived(gx_half(slot, half), r.gx_r.at[slot, half])
+
+    gx_send(t, 0, 1, 1)
+    gx_send(t, 1, 3, 2)
+    gx_send(t, 1, 1, 3)
+    gx_send(t, 0, 3, 8)
+    start(remote(r.gx.at[t], r.gx.at[t], r.gx_s.at[0], r.gx_r.at[t, 0], d, mate))
 
     def wkv_send(slot, half, dp, index):
         ref = r.wkv.at[slot, half]
@@ -258,6 +271,13 @@
         return remote(r.c0.at[d], r.c0.at[d], r.c0_s.at[0], r.c0_r.at[0], peer, t)
 
     over_dp(lambda k, peer: c0_copy(k, peer).start())
+
+    before = turn(zh, 3, 4) * 2 + c
+    after = turn(zh, 1, 4) * 2 + c
+    gx_arrived(before, 0)
+    gx_send(before, 0, 1, 9)
+    gx_arrived(after, 1)
+    gx_send(after, 1, 3, 10)
 
     def wkv_second(first, k_list):
         for k in k_list:
@@ -286,17 +306,19 @@
 
     sums, square = project(t, jnp.zeros((64, 768), F32), jnp.zeros((64, 1), F32))
 
-    for k in (1, 3, 2):
+    for k, halves in ((1, (0,)), (3, (1,)), (2, (0, 1))):
         slot = turn(zh, k, 4) * 2 + c
-        arrived(r.gx.at[slot], r.gx_r.at[slot])
-        start(remote(r.gx.at[slot], r.gx.at[slot], r.gx_s.at[4 + k], r.gx_r.at[slot], d, mate))
+        for half in halves:
+            gx_arrived(slot, half)
+        ref = r.gx.at[slot]
+        start(remote(ref, ref, r.gx_s.at[4 + k], r.gx_r.at[slot, 0], d, mate))
         sums, square = project(slot, sums, square)
 
-    arrived(r.gx.at[mate], r.gx_r.at[mate])
+    arrived(r.gx.at[mate], r.gx_r.at[mate, 0])
     sums, square = project(mate, sums, square)
     for k in (1, 3, 2):
         slot = turn(zh, k, 4) * 2 + (1 - c)
-        arrived(r.gx.at[slot], r.gx_r.at[slot])
+        arrived(r.gx.at[slot], r.gx_r.at[slot, 0])
         sums, square = project(slot, sums, square)
 
     length = r.cap_len[0]

time: 92 us -> 91.9 us (level)
  no operation moved by 1% of the time
where the time goes in v7:
time: 91.9 us; the launch traced here: 91.7 us
  Pallas kernels  89.2 us (97%)
  between operations  2.58 us (3%)
    pallas_call x1, Pallas kernels, local(): pl.pallas_call(kernel, out_shape=[jax.ShapeDtypeStruct((1, 128), F32), ja...  87.4 us

profile of v7, /device:TPU:1, one launch (start us, length us, event | category | flops | bytes accessed | tf_op | source)
XLA Modules:
  0.0 91.7 jit_solution(11229134110291581008)
XLA Ops:
  2.6 87.4 %motion_block.1 = (f32[1,128]{1,0:T(1,128)}, f32[384,256]{1,0:T(8,128)}) custom-call(bf16[1,64,512]{2,1,0:T(8,128)(2,1)} %refs_0_.1, s32[1]{0:T(128)S(6)} %copy.26.refs_1_, s32[1]{0:T(128)S(6)} %copy.27.refs_2_, s32[1]{0:T(128)S(6)} %copy.28.refs_3_, f32[8,1,512]{2,1,0:T(1,128)} %bitcast.10, f32[1,128]{1,0:T(1,128)} %bitcast.11, f32[1,128]{1,0:T(1,128)} %bitcast.12, ...), custom_call_target="tpu_custom_call" | custom-call | tf_op jit(solution)/shard_map/motion_block/pallas_call | solution.py:801
  90.0 1.7 %unpack.1 = (f32[1,128]{1,0:T(1,128)}, f32[64,256]{1,0:T(8,128)}, f32[128,256]{1,0:T(8,128)}, f32[128,256]{1,0:T(8,128)}, f32[64,256]{1,0:T(8,128)}) custom-call(f32[1,128]{1,0:T(1,128)} %get-tuple-element.12.loss, f32[384,256]{1,0:T(8,128)} %get-tuple-element.13.packed), custom_call_target="tpu_custom_call" | custom-call | tf_op jit(solution)/shard_map/unpack/pallas_call | solution.py:841

commit v8 on v6

--- a/solution.py
+++ b/solution.py
@@ -214,6 +214,20 @@
     for half in (0, 1):
         r.wkv[xy, half, :, 0:256] = wk_v[64 * half : 64 * half + 64]
         r.wkv[xy, half, :, 256:512] = wv_v[64 * half : 64 * half + 64]
+    pl.semaphore_wait(barrier, 38)
+
+    for k in (2, 1, 3):
+        start(remote(r.gx.at[t], r.gx.at[t], r.gx_s.at[k], r.gx_r.at[t], d, turn(zh, k, 4) * 2 + c))
+    start(remote(r.gx.at[t], r.gx.at[t], r.gx_s.at[0], r.gx_r.at[t], d, mate))
+
+    def wkv_send(slot, half, dp, index):
+        ref = r.wkv.at[slot, half]
+        start(remote(ref, ref, r.wkv_s.at[index], r.wkv_r.at[slot, half], dp, t))
+
+    for k in (1, 3, 2):
+        wkv_send(xy, 0, plane(turn(x, k, 4), y), k - 1)
+        wkv_send(xy, 1, plane(x, turn(y, k, 4)), 2 + k)
+
     w_in_v = r.w_in[...]
     w_in_t = w_in_v.astype(F32)
     decay = -math.log(10000.0) / 1024.0
@@ -239,20 +253,6 @@
     wq_v = r.wq[...]
     part_m = tn(r.wo[...], vel_v).reshape(32, 8, 256)
     part_b = tn(w_in_v, vel_v)
-
-    pl.semaphore_wait(barrier, 38)
-
-    for k in (2, 1, 3):
-        start(remote(r.gx.at[t], r.gx.at[t], r.gx_s.at[k], r.gx_r.at[t], d, turn(zh, k, 4) * 2 + c))
-    start(remote(r.gx.at[t], r.gx.at[t], r.gx_s.at[0], r.gx_r.at[t], d, mate))
-
-    def wkv_send(slot, half, dp, index):
-        ref = r.wkv.at[slot, half]
-        start(remote(ref, ref, r.wkv_s.at[index], r.wkv_r.at[slot, half], dp, t))
-
-    for k in (1, 3, 2):
-        wkv_send(xy, 0, plane(turn(x, k, 4), y), k - 1)
-        wkv_send(xy, 1, plane(x, turn(y, k, 4)), 2 + k)
 
     def c0_copy(k, peer):
         return remote(r.c0.at[d], r.c0.at[d], r.c0_s.at[0], r.c0_r.at[0], peer, t)

time: 92 us -> 92 us (level)
  no operation moved by 1% of the time
where the time goes in v8:
time: 92 us; the launch traced here: 91.8 us
  Pallas kernels  89.3 us (97%)
  between operations  2.58 us (3%)
    pallas_call x1, Pallas kernels, local(): pl.pallas_call(kernel, out_shape=[jax.ShapeDtypeStruct((1, 128), F32), ja...  87.5 us

profile of v8, /device:TPU:1, one launch (start us, length us, event | category | flops | bytes accessed | tf_op | source)
XLA Modules:
  0.0 91.8 jit_solution(12090748921827112737)
XLA Ops:
  2.6 87.5 %motion_block.1 = (f32[1,128]{1,0:T(1,128)}, f32[384,256]{1,0:T(8,128)}) custom-call(bf16[1,64,512]{2,1,0:T(8,128)(2,1)} %refs_0_.1, s32[1]{0:T(128)S(6)} %copy.26.refs_1_, s32[1]{0:T(128)S(6)} %copy.27.refs_2_, s32[1]{0:T(128)S(6)} %copy.28.refs_3_, f32[8,1,512]{2,1,0:T(1,128)} %bitcast.10, f32[1,128]{1,0:T(1,128)} %bitcast.11, f32[1,128]{1,0:T(1,128)} %bitcast.12, ...), custom_call_target="tpu_custom_call" | custom-call | tf_op jit(solution)/shard_map/motion_block/pallas_call | solution.py:779
  90.1 1.7 %unpack.1 = (f32[1,128]{1,0:T(1,128)}, f32[64,256]{1,0:T(8,128)}, f32[128,256]{1,0:T(8,128)}, f32[128,256]{1,0:T(8,128)}, f32[64,256]{1,0:T(8,128)}) custom-call(f32[1,128]{1,0:T(1,128)} %get-tuple-element.12.loss, f32[384,256]{1,0:T(8,128)} %get-tuple-element.13.packed), custom_call_target="tpu_custom_call" | custom-call | tf_op jit(solution)/shard_map/unpack/pallas_call | solution.py:819

commit v9 on v8

--- a/solution.py
+++ b/solution.py
@@ -433,26 +433,6 @@
     start(remote(r.pzb.at[zl], r.pzb.at[zl], r.pb_s.at[0], r.pb_r.at[0], other, t))
     start(remote(r.pzf.at[zl], r.pzf.at[zl], r.pf_s.at[0], r.pf_r.at[0], other, t))
 
-    for k in (0, 1, 2, 3):
-        for j in (1, 2, 3):
-            slot = turn(x, k, 4) * 4 + turn(y, j, 4)
-            arrived(r.wkv.at[slot, 0], r.wkv_r.at[slot, 0])
-            slot = turn(x, j, 4) * 4 + turn(y, k, 4)
-            arrived(r.wkv.at[slot, 1], r.wkv_r.at[slot, 1])
-
-    forwards = []
-    for z in (0, 1):
-        for near in (0, 1):
-            chunk = near * 2 + c
-            ref = r.caps.at[chunk, z]
-            own_slot = inside & (chunk == mine) & (z == zl)
-
-            @pl.when(jnp.logical_not(own_slot))
-            def _(ref=ref, chunk=chunk, z=z):
-                arrived(ref, r.cp_r.at[chunk, z])
-
-            start(remote(ref, ref, r.cp_s.at[4 + 2 * z + near], r.cp_r.at[chunk, z], d, mate))
-
     arrived(r.pzb.at[1 - zl], r.pb_r.at[0])
     arrived(r.pzf.at[1 - zl], r.pf_r.at[0])
     r.agb[xy] = (plane_b + r.pzb[1 - zl].astype(F32)).astype(BF16)
@@ -468,6 +448,26 @@
         remote(r.agf.at[c, xy], r.agf.at[c, xy], r.af_s.at[0], r.af_r.at[0], dp, t).start()
 
     over_plane(a_start)
+
+    for k in (0, 1, 2, 3):
+        for j in (1, 2, 3):
+            slot = turn(x, k, 4) * 4 + turn(y, j, 4)
+            arrived(r.wkv.at[slot, 0], r.wkv_r.at[slot, 0])
+            slot = turn(x, j, 4) * 4 + turn(y, k, 4)
+            arrived(r.wkv.at[slot, 1], r.wkv_r.at[slot, 1])
+
+    forwards = []
+    for z in (0, 1):
+        for near in (0, 1):
+            chunk = near * 2 + c
+            ref = r.caps.at[chunk, z]
+            own_slot = inside & (chunk == mine) & (z == zl)
+
+            @pl.when(jnp.logical_not(own_slot))
+            def _(ref=ref, chunk=chunk, z=z):
+                arrived(ref, r.cp_r.at[chunk, z])
+
+            start(remote(ref, ref, r.cp_s.at[4 + 2 * z + near], r.cp_r.at[chunk, z], d, mate))
 
     def project_caption(chunk):
         rows = r.caps[chunk].reshape(128, 512)

time: 92 us -> 90.4 us (0.983)
  Pallas kernels: 89.3 us -> 87.6 us
    pallas_call x1, Pallas kernels: 87.5 us -> 85.9 us  [local(): pl.pallas_call(kernel, out_shape=[jax.ShapeDtypeStruct((1, 128), F32), ja...]
where the time goes in v9:
time: 90.4 us; the launch traced here: 90.2 us
  Pallas kernels  87.6 us (97%)
  between operations  2.58 us (3%)
    pallas_call x1, Pallas kernels, local(): pl.pallas_call(kernel, out_shape=[jax.ShapeDtypeStruct((1, 128), F32), ja...  85.9 us

profile of v9, /device:TPU:1, one launch (start us, length us, event | category | flops | bytes accessed | tf_op | source)
XLA Modules:
  0.0 90.2 jit_solution(7150420212384043231)
XLA Ops:
  2.6 85.9 %motion_block.1 = (f32[1,128]{1,0:T(1,128)}, f32[384,256]{1,0:T(8,128)}) custom-call(bf16[1,64,512]{2,1,0:T(8,128)(2,1)} %refs_0_.1, s32[1]{0:T(128)S(6)} %copy.26.refs_1_, s32[1]{0:T(128)S(6)} %copy.27.refs_2_, s32[1]{0:T(128)S(6)} %copy.28.refs_3_, f32[8,1,512]{2,1,0:T(1,128)} %bitcast.10, f32[1,128]{1,0:T(1,128)} %bitcast.11, f32[1,128]{1,0:T(1,128)} %bitcast.12, ...), custom_call_target="tpu_custom_call" | custom-call | tf_op jit(solution)/shard_map/motion_block/pallas_call | solution.py:779
  88.5 1.7 %unpack.1 = (f32[1,128]{1,0:T(1,128)}, f32[64,256]{1,0:T(8,128)}, f32[128,256]{1,0:T(8,128)}, f32[128,256]{1,0:T(8,128)}, f32[64,256]{1,0:T(8,128)}) custom-call(f32[1,128]{1,0:T(1,128)} %get-tuple-element.12.loss, f32[384,256]{1,0:T(8,128)} %get-tuple-element.13.packed), custom_call_target="tpu_custom_call" | custom-call | tf_op jit(solution)/shard_map/unpack/pallas_call | solution.py:819
